TPU v7x, 128 devices: a whole 4x4x4 slice. The times are simulated.
128 devices in a mesh: replica: 8 (over x_hi, y), fsdp: 16 (over z, x_lo, core).
Axes of the slice: x: 4 (x_hi: 2, x_lo: 2; x = x_hi * 2 + x_lo), y: 4, z: 4, core: 2. Of those that a mesh axis runs over, the one named last changes fastest.
Arguments:
- local_weights: float32 [8, 16384, 2048], P('replica', 'fsdp'), may hold values from -25 to 25
- anchor: bfloat16 [16384, 2048], P('fsdp'), may hold values from -5 to 5
- outer_weights: float32 [16384, 2048], P('replica', 'fsdp'), may hold values from -5 to 5
- momentum: float32 [16384, 2048], P('replica', 'fsdp'), may hold values from -0.6 to 0.6
Outputs:
- new_outer: float32 [16384, 2048], P('replica', 'fsdp')
- new_momentum: float32 [16384, 2048], P('replica', 'fsdp')
- blended: float32 [8, 16384, 2048], P('replica', 'fsdp')
All inputs are finite; a program needn't handle non-finite values.
Results may differ from a plain program's by a relative error of at most 0.0049.
Values may be sent and summed in bfloat16 or wider, within the bound.
A program may use at most 128 MiB of HBM per device.

v0:
```python
import jax
import jax.numpy as jnp
from jax import lax
from jax.sharding import PartitionSpec as P

QB = 128


CLIP_RMS = 0.1
OUTER_RATE = 0.7
MOMENTUM_RATE = 0.9
LEVELS = 127.0


def block_scales(values, block_size):
    rows_here, row_width = values.shape
    grouped = values.reshape(rows_here, row_width // block_size, block_size)
    largest = jnp.max(jnp.abs(grouped), axis=2) + 1e-06
    return (largest / LEVELS).astype(jnp.bfloat16)


def dequantize(quantized, scales, block_size):
    lead_shape = quantized.shape[:-1]
    shaped = quantized.reshape(lead_shape + (quantized.shape[-1] // block_size, block_size)).astype(
        jnp.float32
    )
    return (shaped * scales.astype(jnp.float32)[..., None]).reshape(quantized.shape)


def on_device(local_weights, anchor, outer_weights, momentum):
    replicas = lax.axis_size("replica")
    shards = lax.axis_size("fsdp")
    local_rows = local_weights[0]
    pseudo = anchor.astype(jnp.float32) - local_rows
    rows_here, row_width = pseudo.shape
    scales_half = block_scales(pseudo, QB)
    scales_wide = lax.optimization_barrier(scales_half).astype(jnp.float32)
    grouped = pseudo.reshape(rows_here, row_width // QB, QB)
    quantized = (
        jnp.floor(grouped / scales_wide[..., None] + 0.5)
        .astype(jnp.bfloat16)
        .reshape(rows_here, row_width)
    )
    column_quant, column_scales = (
        lax.all_to_all(quantized, "fsdp", split_axis=1, concat_axis=0, tiled=True),
        lax.all_to_all(scales_half, "fsdp", split_axis=1, concat_axis=0, tiled=True),
    )
    summed = lax.psum_scatter(
        dequantize(column_quant, column_scales, QB), "replica", scatter_dimension=0, tiled=True
    )
    average = summed / replicas
    squares = lax.psum(jnp.sum(average * average), ("replica", "fsdp"))
    entries = average.size * replicas * shards
    factor = jnp.minimum(1.0, CLIP_RMS / jnp.sqrt(squares / entries + 1e-06))
    clipped = average * factor
    new_momentum = MOMENTUM_RATE * momentum + clipped
    new_outer = outer_weights - OUTER_RATE * (clipped + MOMENTUM_RATE * new_momentum)
    outer_half = new_outer.astype(jnp.bfloat16)
    stacked = lax.all_gather(outer_half, "replica", axis=0, tiled=True)
    returned = lax.all_to_all(stacked, "fsdp", split_axis=0, concat_axis=1, tiled=True)
    blended = 0.5 * local_rows + 0.5 * returned.astype(jnp.float32)
    return (new_outer, new_momentum, blended[None])


def solution(mesh):
    placed = (
        P("replica", "fsdp", None),
        P("fsdp", None),
        P("replica", "fsdp"),
        P("replica", "fsdp"),
    )
    return jax.shard_map(
        on_device,
        mesh=mesh,
        in_specs=placed,
        out_specs=(P("replica", "fsdp"), P("replica", "fsdp"), P("replica", "fsdp", None)),
        check_vma=False,
    )
```

profile of v0, /device:TPU:1, one launch (start us, length us, event | category | flops | bytes accessed | tf_op | source)
XLA Modules:
  0.0 455.5 jit_solution(17654768897626765752)
XLA Ops:
  7.2 5.9 %abs_bitcast_fusion = f32[128,8,16,128]{3,1,2,0:T(8,128)S(1)} fusion(f32[1,1024,2048]{2,1,0:T(8,128)} %param.4, bf16[1024,2048]{1,0:T(8,128)(2,1)} %param.5), kind=kLoop, calls=%fused_computation.8 | loop fusion | flops 6291456 | bytes 20971520
  13.0 5.4 %copy.20 = f32[128,8,16,128]{3,2,1,0:T(8,128)} copy(f32[128,8,16,128]{3,1,2,0:T(8,128)S(1)} %abs_bitcast_fusion) | data formatting | bytes 16777216
  18.4 5.6 %reduce_max.9 = f32[1024,16]{1,0:T(8,128)S(1)} reduce(f32[1024,16,128]{2,1,0:T(8,128)} %bitcast.51, f32[]{:T(128)} %constant.11.clone.1), dimensions={2}, to_apply=%region_0.0 | reduce | flops 2080768 | bytes 8454148 | tf_op jit(solution)/shard_map/reduce_max | solution.py:18
  24.1 0.1 fusion.6
  24.2 0.2 copy.15
  24.4 0.5 broadcast.42
  24.9 0.8 reduce
  25.7 0.6 reshape.82
  26.3 7.8 %all-to-all-start.1 = ((bf16[16,2,512]{2,1,0:T(2,128)(2,1)}), bf16[16,2,512]{2,1,0:T(2,128)(2,1)S(1)}, u32[]{:S(2)}, u32[]{:S(2)}) async-start(bf16[16,2,512]{2,1,0:T(2,128)(2,1)} %reshape.82), calls=%async_computation.1 | async-start | bytes 65536 | tf_op jit(solution)/shard_map/all_to_all | solution.py:46
  34.1 0.1 multiply_convert_fusion
  34.2 2.3 div.31
  36.5 8.7 %copy_bitcast_fusion = bf16[1024,16,128]{2,0,1:T(8,128)(2,1)} fusion(f32[128,8,16,128]{3,2,1,0:T(8,128)S(1)} %bitcast.50, f32[1,1024,2048]{2,1,0:T(8,128)} %param.4, bf16[1024,2048]{1,0:T(8,128)(2,1)S(1)} %copy-done), kind=kLoop, calls=%fused_computation.9 | loop fusion | flops 12582912 | bytes 25165824 | tf_op jit(solution)/shard_map/all_to_all | solution.py:45
  45.2 5.7 %all-to-all-start = ((bf16[1024,16,128]{2,0,1:T(8,128)(2,1)}), bf16[1024,16,128]{2,0,1:T(8,128)(2,1)}, u32[]{:S(2)}, u32[]{:S(2)}) async-start(bf16[1024,16,128]{2,0,1:T(8,128)(2,1)} %copy_bitcast_fusion), calls=%async_computation | async-start | bytes 8388608 | tf_op jit(solution)/shard_map/all_to_all | solution.py:45
  50.9 0.0 reduce-scatter.2.cloned.1.call-start
  51.0 0.1 bitcast_convert_fusion
  51.1 49.5 %all-to-all-done = bf16[1024,16,128]{2,0,1:T(8,128)(2,1)} async-done(((bf16[1024,16,128]{2,0,1:T(8,128)(2,1)}), bf16[1024,16,128]{2,0,1:T(8,128)(2,1)}, u32[]{:S(2)}, u32[]{:S(2)}) %all-to-all-start) | async-done | bytes 4194336 | tf_op jit(solution)/shard_map/all_to_all | solution.py:45
  100.6 7.0 %bitcast_multiply_fusion = f32[16384,128]{1,0:T(8,128)} fusion(f32[16384]{0:T(1024)S(1)} %bitcast.53, bf16[1024,16,128]{2,0,1:T(8,128)(2,1)} %all-to-all-done), kind=kLoop, calls=%fused_computation.6 | loop fusion | flops 4194304 | bytes 12648448 | tf_op jit(solution)/shard_map/mul | solution.py:27
  107.6 0.0 reduce-scatter.2.cloned.1.call-update
  107.7 0.0 all-gather.2.cloned.1.call-start
  107.7 113.5 %reduce-scatter.2.cloned.1.call-done = f32[2048,128]{1,0:T(8,128)} async-done(((f32[16384,128]{1,0:T(8,128)}), f32[2048,128]{1,0:T(8,128)}) %reduce-scatter.2.cloned.1.call-update) | async-done | bytes 1048592 | tf_op jit(solution)/shard_map/reduce_scatter | solution.py:48
  221.2 2.1 multiply_reduce_fusion
  223.3 65.0 %psum.7 = f32[]{:T(128)} all-reduce(f32[]{:T(128)} %multiply_reduce_fusion), channel_id=1, replica_groups=mesh['replica'=8,'fsdp'=16] {'replica','fsdp'}, use_global_device_ids=true, to_apply=%region_3.0 | all-reduce | flops 1 | bytes 8 | tf_op jit(solution)/shard_map/psum | solution.py:52
  289.0 3.0 fusion.5
  292.0 0.0 all-gather.2.cloned.1.call-update
  292.0 67.4 %all-gather.2.cloned.1.call-done = bf16[16384,128]{1,0:T(8,128)(2,1)} async-done(((bf16[2048,128]{1,0:T(8,128)(2,1)}), bf16[16384,128]{1,0:T(8,128)(2,1)}) %all-gather.2.cloned.1.call-update) | async-done | bytes 4194320 | tf_op jit(solution)/shard_map/all_gather | solution.py:59
  359.4 5.5 %all-to-all-start.2 = ((bf16[16,1024,128]{2,1,0:T(8,128)(2,1)}), bf16[16,1024,128]{2,1,0:T(8,128)(2,1)}, u32[]{:S(2)}, u32[]{:S(2)}) async-start(bf16[16,1024,128]{2,1,0:T(8,128)(2,1)} %bitcast.52), calls=%async_computation.3 | async-start | bytes 8388608 | tf_op jit(solution)/shard_map/all_to_all | solution.py:60
  365.0 9.2 %copy.17 = f32[1,1024,2048]{1,2,0:T(8,128)} copy(f32[1,1024,2048]{2,1,0:T(8,128)} %param.4) | data formatting | bytes 16777216 | tf_op args[0]
  374.2 40.4 %all-to-all-done.2 = bf16[16,1024,128]{2,1,0:T(8,128)(2,1)} async-done(((bf16[16,1024,128]{2,1,0:T(8,128)(2,1)}), bf16[16,1024,128]{2,1,0:T(8,128)(2,1)}, u32[]{:S(2)}, u32[]{:S(2)}) %all-to-all-start.2) | async-done | bytes 4194336 | tf_op jit(solution)/shard_map/all_to_all | solution.py:60
  414.6 6.4 %copy.16 = bf16[16,1024,128]{1,2,0:T(8,128)(2,1)} copy(bf16[16,1024,128]{2,1,0:T(8,128)(2,1)} %all-to-all-done.2) | data formatting | bytes 8388608 | tf_op jit(solution)/shard_map/all_to_all | solution.py:60
  421.0 6.5 %convert_element_type.89 = f32[16,1024,128]{1,2,0:T(8,128)} convert(bf16[16,1024,128]{1,2,0:T(8,128)(2,1)} %copy.16) | non-fusion elementwise | flops 2097152 | bytes 12582912 | tf_op jit(solution)/shard_map/convert_element_type | solution.py:61
  427.5 12.0 %fusion.3 = f32[1,1024,2048]{1,2,0:T(8,128)} fusion(f32[1,1024,2048]{1,2,0:T(8,128)} %copy.17, f32[1,1024,2048]{1,2,0:T(8,128)} %bitcast.49), kind=kLoop, calls=%fused_computation.5 | loop fusion | flops 4194304 | bytes 25165824 | tf_op jit(solution)/shard_map/add | solution.py:61
  439.5 9.1 %copy.18 = f32[1,1024,2048]{2,1,0:T(8,128)} copy(f32[1,1024,2048]{1,2,0:T(8,128)} %fusion.3) | data formatting | bytes 16777216
  (8 shorter events, 0.0 us)
Async XLA Ops:
  26.3 18.9 %all-to-all-start.1 = ((bf16[16,2,512]{2,1,0:T(2,128)(2,1)}), bf16[16,2,512]{2,1,0:T(2,128)(2,1)S(1)}, u32[]{:S(2)}, u32[]{:S(2)}) async-start(bf16[16,2,512]{2,1,0:T(2,128)(2,1)} %reshape.82), calls=%async_computation.1 | async-start | bytes 65536 | tf_op jit(solution)/shard_map/all_to_all | solution.py:46
  34.1 2.4 copy-start
  45.2 55.4 %all-to-all-start = ((bf16[1024,16,128]{2,0,1:T(8,128)(2,1)}), bf16[1024,16,128]{2,0,1:T(8,128)(2,1)}, u32[]{:S(2)}, u32[]{:S(2)}) async-start(bf16[1024,16,128]{2,0,1:T(8,128)(2,1)} %copy_bitcast_fusion), calls=%async_computation | async-start | bytes 8388608 | tf_op jit(solution)/shard_map/all_to_all | solution.py:45
  50.9 170.3 %reduce-scatter.2.cloned.1.call-start = ((), (), s32[]{:S(2)}) async-start(), calls=%async_computation.4 | async-start | bytes 9437184 | tf_op jit(solution)/shard_map/reduce_scatter | solution.py:48
  100.6 188.4 %copy-start.1 = (f32[2048,128]{1,0:T(8,128)S(1)}, f32[2048,128]{1,0:T(8,128)}, u32[]{:S(2)}) copy-start(f32[2048,128]{1,0:T(8,128)} %param.6) | copy-start | bytes 3145732
  100.6 188.4 %copy-start.2 = (f32[2048,128]{1,0:T(8,128)S(1)}, f32[2048,128]{1,0:T(8,128)}, u32[]{:S(2)}) copy-start(f32[2048,128]{1,0:T(8,128)} %param.7) | copy-start | bytes 3145732
  107.7 251.8 %all-gather.2.cloned.1.call-start = ((), (), s32[]{:S(2)}) async-start(), calls=%async_computation.5 | async-start | bytes 4718592 | tf_op jit(solution)/shard_map/all_gather | solution.py:59
  359.4 55.2 %all-to-all-start.2 = ((bf16[16,1024,128]{2,1,0:T(8,128)(2,1)}), bf16[16,1024,128]{2,1,0:T(8,128)(2,1)}, u32[]{:S(2)}, u32[]{:S(2)}) async-start(bf16[16,1024,128]{2,1,0:T(8,128)(2,1)} %bitcast.52), calls=%async_computation.3 | async-start | bytes 8388608 | tf_op jit(solution)/shard_map/all_to_all | solution.py:60
Sparse Core Ops, SparseCore 0:
  107.8 113.4 reduce-scatter.1
  292.1 67.2 all-gather.1
where the time goes:
time: 456 us; the launch traced here: 455 us
  waiting for transfers between devices  271 us (59%)
  blocking collectives  65 us (14%)
  other arithmetic  51.8 us (11%)
  local copies, waits for them, and re-layouts  33.8 us (7%)
  starting transfers between devices  19.1 us (4%)
  between operations  14.8 us (3%)
    reduce_scatter x1, waiting for transfers between devices, on_device(): lax.psum_scatter(dequantize(column_quant, column_scales, QB), 'replica',...  114 us
    all_gather x1, waiting for transfers between devices, on_device(): stacked = lax.all_gather(outer_half, 'replica', axis=0, tiled=True)  67.4 us
    psum x1, blocking collectives, on_device(): squares = lax.psum(jnp.sum(average * average), ('replica', 'fsdp'))  65 us
    all_to_all x1, waiting for transfers between devices, on_device(): lax.all_to_all(quantized, 'fsdp', split_axis=1, concat_axis=0, tiled=True)  49.5 us
    all_to_all x1, waiting for transfers between devices, on_device(): lax.all_to_all(stacked, 'fsdp', split_axis=0, concat_axis=1, tiled=True)  40.4 us
    unnamed x12, local copies, waits for them, and re-layouts  24.9 us
    add x1, other arithmetic, on_device(): blended = 0.5 * local_rows + 0.5 * returned.astype(jnp.float32)  12 us
  transfers between devices with their start and end apart: 5, of which 4 were waited for; matrix products, arithmetic and copies ran while one was open for 4% of the time, Pallas kernels for 0%

commit v1 on v0

v1 whole, which is shorter than its diff:
```python
import jax
import jax.numpy as jnp
from jax import lax
from jax.experimental import pallas as pl
from jax.experimental.pallas import tpu as pltpu
from jax.sharding import PartitionSpec as P

MESH = pl.DeviceIdType.MESH
BF16 = jnp.bfloat16
F32 = jnp.float32

QB = 128
CLIP_RMS = 0.1
OUTER_RATE = 0.7
MOMENTUM_RATE = 0.9
LEVELS = 127.0

NR = 8
NF = 16
PIECE = 128
HALF = 64
QUARTER = 32
LOOKAHEAD = 4


def kernel(
    loc_h, anc_h, ow_h, mo_h,
    no_h, nm_h, bl_h,
    loc, anc, dq, ra, relb, finb, rela, fina, xb, tot, toth, g,
    u, w, ow, mo, oh, t, obuf, part, s1, part2, s2,
    ld, iosem, osem, ss, rs, zs_sem, zr_sem, ps_sem, pr_sem, as_sem, ar_sem,
):
    rows, width = dq.shape
    r = lax.axis_index("replica")
    f = lax.axis_index("fsdp")
    xh, y = r // 4, r % 4
    z, xl, c = f // 4, (f // 2) % 2, f % 2
    plane = r * 4 + xl * 2 + c
    yl, yr, yo = (y + 3) % 4, (y + 1) % 4, (y + 2) % 4
    left = (xh * 4 + yl, f)
    right = (xh * 4 + yr, f)
    across = ((1 - xh) * 4 + y, f)

    def row(x_of, y_of, side, offset=0):
        return pl.multiple_of((4 * x_of + y_of) * PIECE + side * HALF + offset, QUARTER)

    barrier = pltpu.get_barrier_semaphore()

    def greet_plane(i, _):
        other = (plane + i) % 32
        pl.semaphore_signal(
            barrier, inc=1, device_id=(other // 4, z * 4 + other % 4), device_id_type=MESH
        )
        return 0

    lax.fori_loop(1, 32, greet_plane, 0)
    for dz in (1, 2, 3):
        pl.semaphore_signal(
            barrier, inc=1, device_id=(r, ((z + dz) % 4) * 4 + xl * 2 + c), device_id_type=MESH
        )

    far = 1 - xh
    units = [
        (far, yo, 1), (far, yo, 0), (far, yr, 1), (far, yl, 1), (far, yr, 0), (xh, yo, 1),
        (far, yl, 0), (xh, yr, 1), (xh, yl, 1), (far, y, 0), (far, y, 1), (xh, yo, 0),
        (xh, yr, 0), (xh, yl, 0), (xh, y, 1), (xh, y, 0),
    ]
    loads = []
    for k, unit in enumerate(units):
        at = pl.ds(row(*unit), HALF)
        loads.append(
            (
                pltpu.make_async_copy(loc_h.at[0, at], loc.at[at], ld.at[2 * k]),
                pltpu.make_async_copy(anc_h.at[at], anc.at[at], ld.at[2 * k + 1]),
            )
        )
    state_in = (
        pltpu.make_async_copy(ow_h, ow, iosem.at[0]),
        pltpu.make_async_copy(mo_h, mo, iosem.at[1]),
    )

    def begin(k):
        for copy in loads[k]:
            copy.start()

    begin(0)
    for copy in state_in:
        copy.start()
    for k in range(1, LOOKAHEAD):
        begin(k)

    def quantize(k):
        for copy in loads[k]:
            copy.wait()
        if k + LOOKAHEAD < len(units):
            begin(k + LOOKAHEAD)
        base = row(*units[k])

        def step(i, _):
            at = pl.ds(pl.multiple_of(base + i * 16, 16), 16)
            pseudo = anc[at, :].astype(F32) - loc[at, :]
            done = []
            for b in range(width // QB):
                block = pseudo[:, b * QB : (b + 1) * QB]
                largest = jnp.max(jnp.abs(block), axis=1, keepdims=True)
                scale = ((largest + 1e-06) / LEVELS).astype(BF16).astype(F32)
                level = jnp.floor(block / scale + 0.5)
                done.append((level * scale).astype(BF16))
            dq[at, :] = jnp.concatenate(done, axis=1)
            return 0

        lax.fori_loop(0, HALF // 16, step, 0)

    def add(dst, dst_base, terms, count):
        def step(i, _):
            value = None
            for ref, base in terms:
                x = ref[pl.ds(pl.multiple_of(base + i * 16, 16), 16), :].astype(F32)
                value = x if value is None else value + x
            dst[pl.ds(pl.multiple_of(dst_base + i * 16, 16), 16), :] = value.astype(dst.dtype)
            return 0

        lax.fori_loop(0, count // 16, step, 0)

    sent = []

    def put(src, dst, device):
        k = len(sent)
        copy = pltpu.make_async_remote_copy(
            src_ref=src, dst_ref=dst, send_sem=ss.at[k], recv_sem=rs.at[k],
            device_id=device, device_id_type=MESH,
        )
        copy.start()
        sent.append(copy)
        return copy

    def prepare(i, _):
        at = pl.ds(pl.multiple_of(i * 128, 128), 128)
        oh[at, :] = (
            ow[at, :] - (OUTER_RATE * MOMENTUM_RATE * MOMENTUM_RATE) * mo[at, :]
        ).astype(BF16)
        return 0

    for copy in state_in:
        copy.wait()
    lax.fori_loop(0, 16, prepare, 0)
    quantize(0)
    pl.semaphore_wait(barrier, 34)

    sides = {"l": left, "r": right}
    fb = [far, xh]
    relb_copies, finb_copies = [[], []], [[], []]

    def send_relay_b(j):
        base = row(fb[j], yo, 1)
        relb_copies[j] = [
            put(dq.at[pl.ds(base, QUARTER)], relb.at[pl.ds(j * 64, QUARTER)], right),
            put(dq.at[pl.ds(base + QUARTER, QUARTER)], relb.at[pl.ds(j * 64 + QUARTER, QUARTER)], left),
        ]

    def send_now(src_base, dst, dst_base, side, offset):
        return put(
            dq.at[pl.ds(src_base + offset, QUARTER)],
            dst.at[pl.ds(dst_base + offset, QUARTER)],
            sides[side],
        )

    ra_copies = []

    def send_a(i, y_of):
        ra_copies.append(put(dq.at[pl.ds(row(far, y_of, 0), HALF)], ra.at[pl.ds(i * HALF, HALF)], across))

    send_relay_b(0)

    def spread(b, _):
        c_of, p = b // 8, b % 8
        src = oh.at[pl.ds(pl.multiple_of(b * 128, 128), 128)]
        dst = t.at[
            pl.ds(pl.multiple_of((r // 2) * 128, 128), 128),
            pl.ds(pl.multiple_of((2 * xl + c) * 128, 128), 128),
        ]
        own = jnp.logical_and(jnp.logical_and(p == r, y % 2 == xl), c_of == c)

        @pl.when(own)
        def _():
            pltpu.make_async_copy(src, dst, pr_sem.at[0]).start()

        @pl.when(jnp.logical_not(own))
        def _():
            pltpu.make_async_remote_copy(
                src_ref=src, dst_ref=dst, send_sem=ps_sem.at[0], recv_sem=pr_sem.at[0],
                device_id=(p, z * 4 + (y % 2) * 2 + c_of), device_id_type=MESH,
            ).start()

        return 0

    lax.fori_loop(0, 16, spread, 0)

    quantize(1)
    send_a(0, yo)
    quantize(2)
    finb_copies[0].append(send_now(row(far, yr, 1), finb, 0, "r", QUARTER))
    quantize(3)
    finb_copies[0].append(send_now(row(far, yl, 1), finb, HALF, "l", 0))
    quantize(4)
    send_a(1, yr)
    quantize(5)
    send_relay_b(1)
    quantize(6)
    send_a(2, yl)

    def relay_b(j):
        for copy in relb_copies[j]:
            copy.wait_recv()
        base = row(fb[j], yr, 1)
        add(dq, base, ((dq, base), (relb, j * 64)), QUARTER)
        finb_copies[j].append(send_now(base, finb, j * 128, "r", 0))
        base = row(fb[j], yl, 1) + QUARTER
        add(dq, base, ((dq, base), (relb, j * 64 + QUARTER)), QUARTER)
        finb_copies[j].append(send_now(base - QUARTER, finb, j * 128 + HALF, "l", QUARTER))

    quantize(7)
    finb_copies[1].append(send_now(row(xh, yr, 1), finb, 128, "r", QUARTER))
    quantize(8)
    finb_copies[1].append(send_now(row(xh, yl, 1), finb, 128 + HALF, "l", 0))
    relay_b(0)
    quantize(9)
    send_a(3, y)
    quantize(10)
    quantize(11)

    def pair(i, y_of):
        ra_copies[i].wait_recv()
        base = row(xh, y_of, 0)
        add(dq, base, ((dq, base), (ra, i * HALF)), HALF)
        return base

    base = pair(0, yo)
    rela_copies = [
        put(dq.at[pl.ds(base, QUARTER)], rela.at[pl.ds(0, QUARTER)], right),
        put(dq.at[pl.ds(base + QUARTER, QUARTER)], rela.at[pl.ds(QUARTER, QUARTER)], left),
    ]
    quantize(12)
    quantize(13)
    relay_b(1)
    quantize(14)
    quantize(15)

    for copy in finb_copies[0]:
        copy.wait_recv()
    base = row(far, y, 1)
    add(dq, base, ((dq, base), (finb, 0), (finb, HALF)), HALF)
    xb_copy = put(dq.at[pl.ds(base, HALF)], xb, across)

    pltpu.make_async_copy(t, t, pr_sem.at[0]).wait()

    def along_z(src_of, dst_of, q):
        for dz in (1, 2, 3):
            z_of = (z + dz) % 4
            pltpu.make_async_remote_copy(
                src_ref=src_of(z_of), dst_ref=dst_of(z), send_sem=zs_sem.at[q], recv_sem=zr_sem.at[q],
                device_id=(r, z_of * 4 + xl * 2 + c), device_id_type=MESH,
            ).start()
        pltpu.make_async_copy(src_of(z), dst_of(z), zr_sem.at[q]).start()

    along_z(
        lambda z_of: t.at[pl.ds(pl.multiple_of(z_of * 128, 128), 128)],
        lambda z_of: obuf.at[:, pl.ds(pl.multiple_of(z_of * 512, 512), 512)],
        0,
    )

    base = pair(1, yr)
    fina_copies = [send_now(base, fina, 0, "r", QUARTER)]
    base = pair(2, yl)
    fina_copies.append(send_now(base, fina, HALF, "l", 0))
    for copy in rela_copies:
        copy.wait_recv()
    base = row(xh, yr, 0)
    add(dq, base, ((dq, base), (rela, 0)), QUARTER)
    fina_copies.append(send_now(base, fina, 0, "r", 0))
    base = row(xh, yl, 0) + QUARTER
    add(dq, base, ((dq, base), (rela, QUARTER)), QUARTER)
    fina_copies.append(send_now(base - QUARTER, fina, HALF, "l", QUARTER))

    def total(tot_base, terms, carry):
        def step(i, carry):
            value = None
            for ref, base in terms:
                x = ref[pl.ds(pl.multiple_of(base + i * 16, 16), 16), :].astype(F32)
                value = x if value is None else value + x
            at = pl.ds(pl.multiple_of(tot_base + i * 16, 16), 16)
            tot[at, :] = value
            toth[at, :] = value.astype(BF16)
            square = value * value
            for a in range(0, 16, 8):
                for b in range(0, width, 128):
                    carry = carry + square[a : a + 8, b : b + 128]
            return carry

        return lax.fori_loop(0, HALF // 16, step, carry)

    for copy in finb_copies[1]:
        copy.wait_recv()
    xb_copy.wait_recv()
    carry = total(
        HALF,
        ((dq, row(xh, y, 1)), (finb, 128), (finb, 128 + HALF), (xb, 0)),
        jnp.zeros((8, 128), F32),
    )
    ra_copies[3].wait_recv()
    for copy in fina_copies:
        copy.wait_recv()
    carry = total(
        0, ((dq, row(xh, y, 0)), (ra, 3 * HALF), (fina, 0), (fina, HALF)), carry
    )

    part[...] = carry
    s1[pl.ds(pl.multiple_of(plane * 8, 8), 8), :] = carry

    def tell_plane(i, _):
        other = (plane + i) % 32
        pltpu.make_async_remote_copy(
            src_ref=part, dst_ref=s1.at[pl.ds(pl.multiple_of(plane * 8, 8), 8)],
            send_sem=as_sem.at[0], recv_sem=ar_sem.at[0],
            device_id=(other // 4, z * 4 + other % 4), device_id_type=MESH,
        ).start()
        return 0

    lax.fori_loop(1, 32, tell_plane, 0)

    along_z(
        lambda z_of: toth.at[:, pl.ds(pl.multiple_of(z_of * 512, 512), 512)],
        lambda z_of: u.at[pl.ds(pl.multiple_of(z_of * 128, 128), 128)],
        1,
    )

    def wait_bytes(ref, sem):
        pltpu.make_async_copy(ref, ref, sem).wait()

    wait_bytes(s1.at[pl.ds(0, 31 * 8)], ar_sem.at[0])
    wait_bytes(s1.at[pl.ds(0, 31 * 8)], as_sem.at[0])
    in_plane = s1[0:8, :]
    for k in range(1, 32):
        in_plane = in_plane + s1[8 * k : 8 * k + 8, :]
    part2[...] = in_plane
    s2[pl.ds(pl.multiple_of(z * 8, 8), 8), :] = in_plane
    for dz in (1, 2, 3):
        z_of = (z + dz) % 4
        pltpu.make_async_remote_copy(
            src_ref=part2, dst_ref=s2.at[pl.ds(pl.multiple_of(z * 8, 8), 8)],
            send_sem=as_sem.at[1], recv_sem=ar_sem.at[1],
            device_id=(r, z_of * 4 + xl * 2 + c), device_id_type=MESH,
        ).start()
    wait_bytes(obuf, zr_sem.at[0])
    wait_bytes(s2.at[pl.ds(0, 24)], ar_sem.at[1])
    wait_bytes(s2.at[pl.ds(0, 24)], as_sem.at[1])
    everywhere = s2[0:8, :] + s2[8:16, :] + s2[16:24, :] + s2[24:32, :]
    squares = jnp.sum(everywhere, keepdims=True)
    entries = float(rows * NF) * width
    mean = squares * (1.0 / (NR * NR * entries))
    factor = jnp.minimum(1.0, CLIP_RMS / jnp.sqrt(mean + 1e-06)) * (1.0 / NR)
    weight = (OUTER_RATE * (1.0 + MOMENTUM_RATE)) * factor

    own = r * PIECE

    def outer_half(base):
        def step(i, _):
            at = pl.ds(pl.multiple_of(base + i * 16, 16), 16)
            g[pl.ds(pl.multiple_of(own + base + i * 16, 16), 16), :] = (
                obuf[at, :].astype(F32) - weight * tot[at, :]
            ).astype(BF16)
            return 0

        lax.fori_loop(0, HALF // 16, step, 0)

    def move(base, count, device):
        at = pl.ds(pl.multiple_of(base, QUARTER), count)
        return put(g.at[at], g.at[at], device)

    def ring(base):
        r0 = move(base, QUARTER, right)
        l1 = move(base + QUARTER, QUARTER, left)
        r1 = move(base + QUARTER, QUARTER, right)
        l0 = move(base, QUARTER, left)
        return r0, l1, r1, l0

    def pass_on(x_of, side, copies):
        r0, l1 = copies[:2]
        r0.wait_recv()
        first = move(row(x_of, yl, side), QUARTER, right)
        l1.wait_recv()
        second = move(row(x_of, yr, side) + QUARTER, QUARTER, left)
        return first, second

    outer_half(HALF)
    over_b = move(row(xh, y, 1), HALF, across)
    outer_half(0)
    ring_a = ring(row(xh, y, 0))
    over_a = [move(row(xh, y, 0), HALF, across)]
    ring_b = ring(row(xh, y, 1))

    wait_bytes(u, zr_sem.at[1])

    def to_owner(b, _):
        z_of, k = b // 4, b % 4
        src = u.at[
            pl.ds(pl.multiple_of(z_of * 128, 128), 128), pl.ds(pl.multiple_of(k * 128, 128), 128)
        ]
        dst = w.at[pl.ds(pl.multiple_of(c * 1024 + r * 128, 128), 128)]
        is_own = jnp.logical_and(2 * z_of + xl == r, k == 2 * xl + c)

        @pl.when(is_own)
        def _():
            pltpu.make_async_copy(src, dst, pr_sem.at[1]).start()

        @pl.when(jnp.logical_not(is_own))
        def _():
            pltpu.make_async_remote_copy(
                src_ref=src, dst_ref=dst, send_sem=ps_sem.at[1], recv_sem=pr_sem.at[1],
                device_id=(2 * z_of + xl, z * 4 + k), device_id_type=MESH,
            ).start()

        return 0

    lax.fori_loop(0, 16, to_owner, 0)

    def blend(base):
        def step(i, _):
            at = pl.ds(pl.multiple_of(base + i * 16, 16), 16)
            loc[at, :] = 0.5 * loc[at, :] + 0.5 * g[at, :].astype(F32)
            return 0

        lax.fori_loop(0, HALF // 16, step, 0)
        at = pl.ds(base, HALF)
        pltpu.make_async_copy(loc.at[at], bl_h.at[0, at], osem.at[2]).start()

    blend(row(xh, y, 1))
    blend(row(xh, y, 0))
    on_a = pass_on(xh, 0, ring_a)
    ring_a[2].wait_recv()
    over_a.append(move(row(xh, yl, 0), HALF, across))
    ring_a[3].wait_recv()
    over_a.append(move(row(xh, yr, 0), HALF, across))
    blend(row(xh, yl, 0))
    blend(row(xh, yr, 0))
    over_b.wait_recv()
    ring_x = ring(row(far, y, 1))
    blend(row(far, y, 1))
    on_b = pass_on(xh, 1, ring_b)
    for copy in on_a:
        copy.wait_recv()
    over_a.append(move(row(xh, yo, 0), HALF, across))
    blend(row(xh, yo, 0))
    for copy in ring_b[2:]:
        copy.wait_recv()
    blend(row(xh, yl, 1))
    blend(row(xh, yr, 1))

    wait_bytes(w, pr_sem.at[1])

    def finish(i, _):
        at = pl.ds(pl.multiple_of(i * 128, 128), 128)
        clipped = factor * w[at, :].astype(F32)
        momentum = MOMENTUM_RATE * mo[at, :] + clipped
        ow[at, :] = ow[at, :] - OUTER_RATE * (clipped + MOMENTUM_RATE * momentum)
        mo[at, :] = momentum
        return 0

    lax.fori_loop(0, 16, finish, 0)
    state_out = (
        pltpu.make_async_copy(ow, no_h, osem.at[0]),
        pltpu.make_async_copy(mo, nm_h, osem.at[1]),
    )
    for copy in state_out:
        copy.start()

    over_a[0].wait_recv()
    blend(row(far, y, 0))
    on_x = pass_on(far, 1, ring_x)
    for copy in on_b:
        copy.wait_recv()
    blend(row(xh, yo, 1))
    for copy in ring_x[2:]:
        copy.wait_recv()
    blend(row(far, yl, 1))
    blend(row(far, yr, 1))
    over_a[1].wait_recv()
    blend(row(far, yl, 0))
    over_a[2].wait_recv()
    blend(row(far, yr, 0))
    for copy in on_x:
        copy.wait_recv()
    blend(row(far, yo, 1))
    over_a[3].wait_recv()
    blend(row(far, yo, 0))

    for copy in sent:
        copy.wait_send()
    wait_bytes(t.at[pl.ds(0, 384)], zs_sem.at[0])
    wait_bytes(u.at[pl.ds(0, 384)], zs_sem.at[1])
    in_place = y % 2 == xl
    for q, ref in ((0, t), (1, u)):

        @pl.when(in_place)
        def _():
            wait_bytes(ref.at[pl.ds(0, 480)], ps_sem.at[q])

        @pl.when(jnp.logical_not(in_place))
        def _():
            wait_bytes(ref, ps_sem.at[q])

    for copy in state_out:
        copy.wait()
    pltpu.make_async_copy(loc, bl_h.at[0], osem.at[2]).wait()


def on_device(local_weights, anchor, outer_weights, momentum):
    _, rows, width = local_weights.shape
    owned, tile = outer_weights.shape
    whole = pl.BlockSpec(memory_space=pl.ANY)
    vmem = pltpu.VMEM
    dma = pltpu.SemaphoreType.DMA
    return pl.pallas_call(
        kernel,
        out_shape=(
            jax.ShapeDtypeStruct((owned, tile), F32),
            jax.ShapeDtypeStruct((owned, tile), F32),
            jax.ShapeDtypeStruct((1, rows, width), F32),
        ),
        in_specs=[whole] * 4,
        out_specs=(whole,) * 3,
        scratch_shapes=[
            vmem((rows, width), F32),
            vmem((rows, width), BF16),
            vmem((rows, width), BF16),
            vmem((4 * HALF, width), BF16),
            vmem((128, width), BF16),
            vmem((256, width), BF16),
            vmem((64, width), BF16),
            vmem((128, width), BF16),
            vmem((HALF, width), BF16),
            vmem((PIECE, width), F32),
            vmem((PIECE, width), BF16),
            vmem((rows, width), BF16),
            vmem((512, 512), BF16),
            vmem((owned, tile), BF16),
            vmem((owned, tile), F32),
            vmem((owned, tile), F32),
            vmem((owned, tile), BF16),
            vmem((512, 512), BF16),
            vmem((PIECE, width), BF16),
            vmem((8, 128), F32),
            vmem((256, 128), F32),
            vmem((8, 128), F32),
            vmem((32, 128), F32),
            dma((32,)),
            dma((2,)),
            dma((3,)),
            dma((64,)),
            dma((64,)),
            dma((2,)),
            dma((2,)),
            dma((2,)),
            dma((2,)),
            dma((2,)),
            dma((2,)),
        ],
        compiler_params=pltpu.CompilerParams(
            collective_id=0, has_side_effects=True, vmem_limit_bytes=56 << 20
        ),
    )(local_weights, anchor, outer_weights, momentum)


def solution(mesh):
    placed = (
        P("replica", "fsdp", None),
        P("fsdp", None),
        P("replica", "fsdp"),
        P("replica", "fsdp"),
    )
    return jax.shard_map(
        on_device,
        mesh=mesh,
        in_specs=placed,
        out_specs=(P("replica", "fsdp"), P("replica", "fsdp"), P("replica", "fsdp", None)),
        check_vma=False,
    )
```

time: 456 us -> 118 us (0.26)
  waiting for transfers between devices: 271 us -> 0 us
  Pallas kernels: 0 us -> 105 us
  blocking collectives: 65 us -> 0 us
  other arithmetic: 51.8 us -> 0 us
  local copies, waits for them, and re-layouts: 33.8 us -> 12.4 us
  starting transfers between devices: 19.1 us -> 0 us
  between operations: 14.8 us -> 0.64 us
    reduce_scatter x1 -> x0, waiting for transfers between devices: 114 us -> none  [on_device(): lax.psum_scatter(dequantize(column_quant, column_scales, QB), 'replica',...]
    pallas_call x0 -> x1, Pallas kernels: none -> 105 us  [on_device(): pl.pallas_call(kernel, out_shape=(jax.ShapeDtypeStruct((owned, tile), F32...]
    all_to_all x3 -> x0, waiting for transfers between devices: 90 us -> none  [the longest x1 49.5 us: on_device(): lax.all_to_all(quantized, 'fsdp', split_axis=1, concat_axis=0, tiled=True)]
    all_gather x1 -> x0, waiting for transfers between devices: 67.4 us -> none  [on_device(): stacked = lax.all_gather(outer_half, 'replica', axis=0, tiled=True)]
    psum x1 -> x0, blocking collectives: 65 us -> none  [on_device(): squares = lax.psum(jnp.sum(average * average), ('replica', 'fsdp'))]
    all_to_all x3 -> x0, starting transfers between devices: 19 us -> none  [the longest x1 7.76 us: on_device(): lax.all_to_all(scales_half, 'fsdp', split_axis=1, concat_axis=0, tiled=True)]
    unnamed x12 -> x3, local copies, waits for them, and re-layouts: 24.9 us -> 12.4 us
    add x1 -> x0, other arithmetic: 12 us -> none  [on_device(): blended = 0.5 * local_rows + 0.5 * returned.astype(jnp.float32)]
  transfers between devices with their start and end apart: 5 -> 0, of which waited for: 4 -> 0; matrix products, arithmetic and copies ran while one was open for 4% -> 0% of each run, Pallas kernels for 0% -> 0%
where the time goes in v1:
time: 118 us
  Pallas kernels  105 us (89%)
  local copies, waits for them, and re-layouts  12.4 us (11%)
    pallas_call x1, Pallas kernels, on_device(): pl.pallas_call(kernel, out_shape=(jax.ShapeDtypeStruct((owned, tile), F32...  105 us
    unnamed x3, local copies, waits for them, and re-layouts  12.4 us

profile of v1, /device:TPU:1, one launch (start us, length us, event | category | flops | bytes accessed | tf_op | source)
XLA Modules:
  0.0 117.6 jit_solution(1613496179372979821)
XLA Ops:
  0.6 104.6 %shard_map.67 = (f32[2048,128]{1,0:T(8,128)}, f32[2048,128]{1,0:T(8,128)}, f32[1,1024,2048]{2,1,0:T(8,128)}) custom-call(f32[1,1024,2048]{2,1,0:T(8,128)} %loc_h.1, bf16[1024,2048]{1,0:T(8,128)(2,1)} %anc_h.1, f32[2048,128]{1,0:T(8,128)} %ow_h.1, f32[2048,128]{1,0:T(8,128)} %mo_h.1), custom_call_target="tpu_custom_call" | custom-call | tf_op jit(solution)/shard_map/pallas_call | solution.py:523
  105.2 2.3 %copy.10 = f32[2048,128]{1,0:T(8,128)} copy(f32[2048,128]{1,0:T(8,128)} %get-tuple-element.6) | data formatting | bytes 2097152
  107.5 2.3 %copy.11 = f32[2048,128]{1,0:T(8,128)} copy(f32[2048,128]{1,0:T(8,128)} %get-tuple-element.7) | data formatting | bytes 2097152
  109.7 7.9 %copy.12 = f32[1,1024,2048]{2,1,0:T(8,128)} copy(f32[1,1024,2048]{2,1,0:T(8,128)} %get-tuple-element.8) | data formatting | bytes 16777216

commit v2 on v1

--- a/solution.py
+++ b/solution.py
@@ -25,17 +25,20 @@
 
 def kernel(
     loc_h, anc_h, ow_h, mo_h,
-    no_h, nm_h, bl_h,
-    loc, anc, dq, ra, relb, finb, rela, fina, xb, tot, toth, g,
-    u, w, ow, mo, oh, t, obuf, part, s1, part2, s2,
-    ld, iosem, osem, ss, rs, zs_sem, zr_sem, ps_sem, pr_sem, as_sem, ar_sem,
+    ow, mo, blended,
+    anc, dq, ra, relb, finb, rela, fina, xb, tot, toth, g,
+    u, w, oh, v, t, obuf, part, s1, part2, s2,
+    ld, iosem, ss, rs, zs_sem, zr_sem, ps_sem, pr_sem, as_sem, ar_sem,
 ):
     rows, width = dq.shape
+    loc = blended.at[0]
     r = lax.axis_index("replica")
     f = lax.axis_index("fsdp")
     xh, y = r // 4, r % 4
     z, xl, c = f // 4, (f // 2) % 2, f % 2
     plane = r * 4 + xl * 2 + c
+    chip = r * 2 + xl
+    column = z * 2 + c
     yl, yr, yo = (y + 3) % 4, (y + 1) % 4, (y + 2) % 4
     left = (xh * 4 + yl, f)
     right = (xh * 4 + yr, f)
@@ -43,21 +46,6 @@
 
     def row(x_of, y_of, side, offset=0):
         return pl.multiple_of((4 * x_of + y_of) * PIECE + side * HALF + offset, QUARTER)
-
-    barrier = pltpu.get_barrier_semaphore()
-
-    def greet_plane(i, _):
-        other = (plane + i) % 32
-        pl.semaphore_signal(
-            barrier, inc=1, device_id=(other // 4, z * 4 + other % 4), device_id_type=MESH
-        )
-        return 0
-
-    lax.fori_loop(1, 32, greet_plane, 0)
-    for dz in (1, 2, 3):
-        pl.semaphore_signal(
-            barrier, inc=1, device_id=(r, ((z + dz) % 4) * 4 + xl * 2 + c), device_id_type=MESH
-        )
 
     far = 1 - xh
     units = [
@@ -89,6 +77,22 @@
     for k in range(1, LOOKAHEAD):
         begin(k)
 
+    barrier = pltpu.get_barrier_semaphore()
+
+    def greet_plane(i, _):
+        other = (plane + i) % 32
+        pl.semaphore_signal(
+            barrier, inc=1, device_id=(other // 4, z * 4 + other % 4), device_id_type=MESH
+        )
+        return 0
+
+    lax.fori_loop(1, 32, greet_plane, 0)
+    for dz in (1, 2, 3):
+        for c_of in (0, 1):
+            pl.semaphore_signal(
+                barrier, inc=1, device_id=(r, ((z + dz) % 4) * 4 + xl * 2 + c_of), device_id_type=MESH
+            )
+
     def quantize(k):
         for copy in loads[k]:
             copy.wait()
@@ -136,7 +140,7 @@
 
     def prepare(i, _):
         at = pl.ds(pl.multiple_of(i * 128, 128), 128)
-        oh[at, :] = (
+        oh[i // 8, i % 4, (i // 4) % 2] = (
             ow[at, :] - (OUTER_RATE * MOMENTUM_RATE * MOMENTUM_RATE) * mo[at, :]
         ).astype(BF16)
         return 0
@@ -145,7 +149,7 @@
         copy.wait()
     lax.fori_loop(0, 16, prepare, 0)
     quantize(0)
-    pl.semaphore_wait(barrier, 34)
+    pl.semaphore_wait(barrier, 37)
 
     sides = {"l": left, "r": right}
     fb = [far, xh]
@@ -172,29 +176,35 @@
 
     send_relay_b(0)
 
-    def spread(b, _):
-        c_of, p = b // 8, b % 8
-        src = oh.at[pl.ds(pl.multiple_of(b * 128, 128), 128)]
-        dst = t.at[
-            pl.ds(pl.multiple_of((r // 2) * 128, 128), 128),
-            pl.ds(pl.multiple_of((2 * xl + c) * 128, 128), 128),
-        ]
-        own = jnp.logical_and(jnp.logical_and(p == r, y % 2 == xl), c_of == c)
-
+    def share(src, dst, q, own, device):
         @pl.when(own)
         def _():
-            pltpu.make_async_copy(src, dst, pr_sem.at[0]).start()
+            pltpu.make_async_copy(src, dst, pr_sem.at[q]).start()
 
         @pl.when(jnp.logical_not(own))
         def _():
             pltpu.make_async_remote_copy(
-                src_ref=src, dst_ref=dst, send_sem=ps_sem.at[0], recv_sem=pr_sem.at[0],
-                device_id=(p, z * 4 + (y % 2) * 2 + c_of), device_id_type=MESH,
+                src_ref=src, dst_ref=dst, send_sem=ps_sem.at[q], recv_sem=pr_sem.at[q],
+                device_id=device, device_id_type=MESH,
             ).start()
 
-        return 0
-
-    lax.fori_loop(0, 16, spread, 0)
+    def spread_y(b):
+        c_of, y_of = b // 4, b % 4
+        share(
+            oh.at[c_of, y_of], v.at[y, :, c], 0,
+            jnp.logical_and(y_of == y, c_of == c), (xh * 4 + y_of, z * 4 + xl * 2 + c_of),
+        )
+
+    def spread_x(b):
+        x_of, y_of = b // 4, b % 4
+        dst = t.at[2 * xh + y_of // 2, xl]
+        share(
+            v.at[y_of, x_of], dst, 2,
+            jnp.logical_and(x_of == xh, y_of % 2 == xl), (x_of * 4 + y, z * 4 + (y_of % 2) * 2 + c),
+        )
+
+    for b in range(8):
+        spread_y(b)
 
     quantize(1)
     send_a(0, yo)
@@ -223,6 +233,9 @@
     finb_copies[1].append(send_now(row(xh, yr, 1), finb, 128, "r", QUARTER))
     quantize(8)
     finb_copies[1].append(send_now(row(xh, yl, 1), finb, 128 + HALF, "l", 0))
+    pltpu.make_async_copy(v, v, pr_sem.at[0]).wait()
+    for b in range(8):
+        spread_x(b)
     relay_b(0)
     quantize(9)
     send_a(3, y)
@@ -252,7 +265,7 @@
     add(dq, base, ((dq, base), (finb, 0), (finb, HALF)), HALF)
     xb_copy = put(dq.at[pl.ds(base, HALF)], xb, across)
 
-    pltpu.make_async_copy(t, t, pr_sem.at[0]).wait()
+    pltpu.make_async_copy(t, t, pr_sem.at[2]).wait()
 
     def along_z(src_of, dst_of, q):
         for dz in (1, 2, 3):
@@ -264,8 +277,8 @@
         pltpu.make_async_copy(src_of(z), dst_of(z), zr_sem.at[q]).start()
 
     along_z(
-        lambda z_of: t.at[pl.ds(pl.multiple_of(z_of * 128, 128), 128)],
-        lambda z_of: obuf.at[:, pl.ds(pl.multiple_of(z_of * 512, 512), 512)],
+        lambda z_of: t.at[z_of],
+        lambda z_of: obuf.at[z_of],
         0,
     )
 
@@ -290,7 +303,10 @@
                 value = x if value is None else value + x
             at = pl.ds(pl.multiple_of(tot_base + i * 16, 16), 16)
             tot[at, :] = value
-            toth[at, :] = value.astype(BF16)
+            for b in range(width // 128):
+                toth[pl.ds(pl.multiple_of(b * PIECE + tot_base + i * 16, 16), 16), :] = value[
+                    :, b * 128 : (b + 1) * 128
+                ].astype(BF16)
             square = value * value
             for a in range(0, 16, 8):
                 for b in range(0, width, 128):
@@ -315,46 +331,48 @@
     )
 
     part[...] = carry
-    s1[pl.ds(pl.multiple_of(plane * 8, 8), 8), :] = carry
+    s1[pl.ds(pl.multiple_of(chip * 8, 8), 8), :] = carry
 
     def tell_plane(i, _):
-        other = (plane + i) % 32
+        other = (chip + i) % 16
         pltpu.make_async_remote_copy(
-            src_ref=part, dst_ref=s1.at[pl.ds(pl.multiple_of(plane * 8, 8), 8)],
+            src_ref=part, dst_ref=s1.at[pl.ds(pl.multiple_of(chip * 8, 8), 8)],
             send_sem=as_sem.at[0], recv_sem=ar_sem.at[0],
-            device_id=(other // 4, z * 4 + other % 4), device_id_type=MESH,
+            device_id=(other // 2, z * 4 + (other % 2) * 2 + c), device_id_type=MESH,
         ).start()
         return 0
 
-    lax.fori_loop(1, 32, tell_plane, 0)
+    lax.fori_loop(1, 16, tell_plane, 0)
 
     along_z(
-        lambda z_of: toth.at[:, pl.ds(pl.multiple_of(z_of * 512, 512), 512)],
-        lambda z_of: u.at[pl.ds(pl.multiple_of(z_of * 128, 128), 128)],
+        lambda z_of: toth.at[pl.ds(pl.multiple_of(z_of * 512, 512), 512)],
+        lambda z_of: u.at[pl.ds(pl.multiple_of(z_of * 512, 512), 512)],
         1,
     )
 
     def wait_bytes(ref, sem):
         pltpu.make_async_copy(ref, ref, sem).wait()
 
-    wait_bytes(s1.at[pl.ds(0, 31 * 8)], ar_sem.at[0])
-    wait_bytes(s1.at[pl.ds(0, 31 * 8)], as_sem.at[0])
+    wait_bytes(s1.at[pl.ds(0, 15 * 8)], ar_sem.at[0])
+    wait_bytes(s1.at[pl.ds(0, 15 * 8)], as_sem.at[0])
     in_plane = s1[0:8, :]
-    for k in range(1, 32):
+    for k in range(1, 16):
         in_plane = in_plane + s1[8 * k : 8 * k + 8, :]
     part2[...] = in_plane
-    s2[pl.ds(pl.multiple_of(z * 8, 8), 8), :] = in_plane
-    for dz in (1, 2, 3):
-        z_of = (z + dz) % 4
+    s2[pl.ds(pl.multiple_of(column * 8, 8), 8), :] = in_plane
+    for d in range(1, 8):
+        other = (column + d) % 8
         pltpu.make_async_remote_copy(
-            src_ref=part2, dst_ref=s2.at[pl.ds(pl.multiple_of(z * 8, 8), 8)],
+            src_ref=part2, dst_ref=s2.at[pl.ds(pl.multiple_of(column * 8, 8), 8)],
             send_sem=as_sem.at[1], recv_sem=ar_sem.at[1],
-            device_id=(r, z_of * 4 + xl * 2 + c), device_id_type=MESH,
+            device_id=(r, (other // 2) * 4 + xl * 2 + other % 2), device_id_type=MESH,
         ).start()
     wait_bytes(obuf, zr_sem.at[0])
-    wait_bytes(s2.at[pl.ds(0, 24)], ar_sem.at[1])
-    wait_bytes(s2.at[pl.ds(0, 24)], as_sem.at[1])
-    everywhere = s2[0:8, :] + s2[8:16, :] + s2[16:24, :] + s2[24:32, :]
+    wait_bytes(s2.at[pl.ds(0, 56)], ar_sem.at[1])
+    wait_bytes(s2.at[pl.ds(0, 56)], as_sem.at[1])
+    everywhere = s2[0:8, :]
+    for k in range(1, 8):
+        everywhere = everywhere + s2[8 * k : 8 * k + 8, :]
     squares = jnp.sum(everywhere, keepdims=True)
     entries = float(rows * NF) * width
     mean = squares * (1.0 / (NR * NR * entries))
@@ -366,9 +384,11 @@
     def outer_half(base):
         def step(i, _):
             at = pl.ds(pl.multiple_of(base + i * 16, 16), 16)
-            g[pl.ds(pl.multiple_of(own + base + i * 16, 16), 16), :] = (
-                obuf[at, :].astype(F32) - weight * tot[at, :]
-            ).astype(BF16)
+            to = pl.ds(pl.multiple_of(own + base + i * 16, 16), 16)
+            for b in range(width // 128):
+                cols = pl.ds(b * 128, 128)
+                state = obuf[b // 4, (b // 2) % 2, b % 2, at, :]
+                g[to, cols] = (state.astype(F32) - weight * tot[at, cols]).astype(BF16)
             return 0
 
         lax.fori_loop(0, HALF // 16, step, 0)
@@ -401,11 +421,9 @@
 
     wait_bytes(u, zr_sem.at[1])
 
-    def to_owner(b, _):
+    def to_owner(b):
         z_of, k = b // 4, b % 4
-        src = u.at[
-            pl.ds(pl.multiple_of(z_of * 128, 128), 128), pl.ds(pl.multiple_of(k * 128, 128), 128)
-        ]
+        src = u.at[pl.ds(b * 128, 128)]
         dst = w.at[pl.ds(pl.multiple_of(c * 1024 + r * 128, 128), 128)]
         is_own = jnp.logical_and(2 * z_of + xl == r, k == 2 * xl + c)
 
@@ -420,9 +438,6 @@
                 device_id=(2 * z_of + xl, z * 4 + k), device_id_type=MESH,
             ).start()
 
-        return 0
-
-    lax.fori_loop(0, 16, to_owner, 0)
 
     def blend(base):
         def step(i, _):
@@ -431,31 +446,51 @@
             return 0
 
         lax.fori_loop(0, HALF // 16, step, 0)
-        at = pl.ds(base, HALF)
-        pltpu.make_async_copy(loc.at[at], bl_h.at[0, at], osem.at[2]).start()
 
     blend(row(xh, y, 1))
+    to_owner(0); to_owner(1)
     blend(row(xh, y, 0))
+    to_owner(2); to_owner(3)
     on_a = pass_on(xh, 0, ring_a)
     ring_a[2].wait_recv()
     over_a.append(move(row(xh, yl, 0), HALF, across))
     ring_a[3].wait_recv()
     over_a.append(move(row(xh, yr, 0), HALF, across))
     blend(row(xh, yl, 0))
+    to_owner(4); to_owner(5)
     blend(row(xh, yr, 0))
+    to_owner(6); to_owner(7)
     over_b.wait_recv()
     ring_x = ring(row(far, y, 1))
     blend(row(far, y, 1))
+    to_owner(8); to_owner(9)
     on_b = pass_on(xh, 1, ring_b)
     for copy in on_a:
         copy.wait_recv()
     over_a.append(move(row(xh, yo, 0), HALF, across))
     blend(row(xh, yo, 0))
+    to_owner(10); to_owner(11)
     for copy in ring_b[2:]:
         copy.wait_recv()
     blend(row(xh, yl, 1))
+    to_owner(12); to_owner(13)
     blend(row(xh, yr, 1))
-
+    to_owner(14); to_owner(15)
+
+    over_a[0].wait_recv()
+    blend(row(far, y, 0))
+    on_x = pass_on(far, 1, ring_x)
+    for copy in on_b:
+        copy.wait_recv()
+    blend(row(xh, yo, 1))
+    for copy in ring_x[2:]:
+        copy.wait_recv()
+    blend(row(far, yl, 1))
+    blend(row(far, yr, 1))
+    over_a[1].wait_recv()
+    blend(row(far, yl, 0))
+    over_a[2].wait_recv()
+    blend(row(far, yr, 0))
     wait_bytes(w, pr_sem.at[1])
 
     def finish(i, _):
@@ -467,27 +502,7 @@
         return 0
 
     lax.fori_loop(0, 16, finish, 0)
-    state_out = (
-        pltpu.make_async_copy(ow, no_h, osem.at[0]),
-        pltpu.make_async_copy(mo, nm_h, osem.at[1]),
-    )
-    for copy in state_out:
-        copy.start()
-
-    over_a[0].wait_recv()
-    blend(row(far, y, 0))
-    on_x = pass_on(far, 1, ring_x)
-    for copy in on_b:
-        copy.wait_recv()
-    blend(row(xh, yo, 1))
-    for copy in ring_x[2:]:
-        copy.wait_recv()
-    blend(row(far, yl, 1))
-    blend(row(far, yr, 1))
-    over_a[1].wait_recv()
-    blend(row(far, yl, 0))
-    over_a[2].wait_recv()
-    blend(row(far, yr, 0))
+
     for copy in on_x:
         copy.wait_recv()
     blend(row(far, yo, 1))
@@ -496,22 +511,19 @@
 
     for copy in sent:
         copy.wait_send()
-    wait_bytes(t.at[pl.ds(0, 384)], zs_sem.at[0])
-    wait_bytes(u.at[pl.ds(0, 384)], zs_sem.at[1])
+    wait_bytes(t.at[pl.ds(0, 3)], zs_sem.at[0])
+    wait_bytes(u.at[pl.ds(0, 1536)], zs_sem.at[1])
+    wait_bytes(u.at[pl.ds(0, 1792)], ps_sem.at[0])
+    wait_bytes(u.at[pl.ds(0, 1536)], ps_sem.at[2])
     in_place = y % 2 == xl
-    for q, ref in ((0, t), (1, u)):
-
-        @pl.when(in_place)
-        def _():
-            wait_bytes(ref.at[pl.ds(0, 480)], ps_sem.at[q])
-
-        @pl.when(jnp.logical_not(in_place))
-        def _():
-            wait_bytes(ref, ps_sem.at[q])
-
-    for copy in state_out:
-        copy.wait()
-    pltpu.make_async_copy(loc, bl_h.at[0], osem.at[2]).wait()
+
+    @pl.when(in_place)
+    def _():
+        wait_bytes(u.at[pl.ds(0, 1920)], ps_sem.at[1])
+
+    @pl.when(jnp.logical_not(in_place))
+    def _():
+        wait_bytes(u, ps_sem.at[1])
 
 
 def on_device(local_weights, anchor, outer_weights, momentum):
@@ -523,14 +535,13 @@
     return pl.pallas_call(
         kernel,
         out_shape=(
-            jax.ShapeDtypeStruct((owned, tile), F32),
-            jax.ShapeDtypeStruct((owned, tile), F32),
-            jax.ShapeDtypeStruct((1, rows, width), F32),
+            vmem((owned, tile), F32),
+            vmem((owned, tile), F32),
+            vmem((1, rows, width), F32),
         ),
         in_specs=[whole] * 4,
-        out_specs=(whole,) * 3,
+        out_specs=(pl.BlockSpec(memory_space=vmem),) * 3,
         scratch_shapes=[
-            vmem((rows, width), F32),
             vmem((rows, width), BF16),
             vmem((rows, width), BF16),
             vmem((4 * HALF, width), BF16),
@@ -540,35 +551,33 @@
             vmem((128, width), BF16),
             vmem((HALF, width), BF16),
             vmem((PIECE, width), F32),
-            vmem((PIECE, width), BF16),
+            vmem((16 * PIECE, 128), BF16),
             vmem((rows, width), BF16),
-            vmem((512, 512), BF16),
+            vmem((16 * PIECE, 128), BF16),
             vmem((owned, tile), BF16),
-            vmem((owned, tile), F32),
-            vmem((owned, tile), F32),
-            vmem((owned, tile), BF16),
-            vmem((512, 512), BF16),
-            vmem((PIECE, width), BF16),
+            vmem((2, 4, 2, PIECE, 128), BF16),
+            vmem((4, 2, 2, PIECE, 128), BF16),
+            vmem((4, 2, 2, PIECE, 128), BF16),
+            vmem((4, 2, 2, PIECE, 128), BF16),
             vmem((8, 128), F32),
-            vmem((256, 128), F32),
+            vmem((128, 128), F32),
             vmem((8, 128), F32),
-            vmem((32, 128), F32),
+            vmem((64, 128), F32),
             dma((32,)),
             dma((2,)),
-            dma((3,)),
             dma((64,)),
             dma((64,)),
             dma((2,)),
             dma((2,)),
-            dma((2,)),
-            dma((2,)),
+            dma((3,)),
+            dma((3,)),
             dma((2,)),
             dma((2,)),
         ],
         compiler_params=pltpu.CompilerParams(
-            collective_id=0, has_side_effects=True, vmem_limit_bytes=56 << 20
+            collective_id=0, has_side_effects=True, vmem_limit_bytes=36 << 20
         ),
-    )(local_weights, anchor, outer_weights, momentum)
+    )(*(pltpu.with_memory_space_constraint(a, pltpu.HBM) for a in (local_weights, anchor, outer_weights, momentum)))
 
 
 def solution(mesh):

time: 118 us -> 100 us (0.85)
  the two profiles are of different devices: /device:TPU:1 before, /device:TPU:25 now
where the time goes in v2:
time: 100 us
  Pallas kernels  94.3 us (94%)
  local copies, waits for them, and re-layouts  5.34 us (5%)
    pallas_call x1, Pallas kernels, on_device(): pl.pallas_call(kernel, out_shape=(vmem((owned, tile), F32), vmem((owned,...  94.3 us
    unnamed x3, local copies, waits for them, and re-layouts  5.34 us

profile of v2, /device:TPU:25, one launch (start us, length us, event | category | flops | bytes accessed | tf_op | source)
XLA Modules:
  0.0 100.3 jit_solution(16194208733719021614)
XLA Ops:
  0.6 94.3 %shard_map.67 = (f32[2048,128]{1,0:T(8,128)S(1)}, f32[2048,128]{1,0:T(8,128)S(1)}, f32[1,1024,2048]{2,1,0:T(8,128)S(1)}) custom-call(f32[1,1024,2048]{2,1,0:T(8,128)} %loc_h.1, bf16[1024,2048]{1,0:T(8,128)(2,1)} %anc_h.1, f32[2048,128]{1,0:T(8,128)} %ow_h.1, f32[2048,128]{1,0:T(8,128)} %mo_h.1), custom_call_target="tpu_custom_call" | custom-call | tf_op jit(solution)/shard_map/pallas_call | solution.py:535
  94.9 1.0 copy.10
  95.9 1.0 copy.11
  96.9 3.4 %copy.12 = f32[1,1024,2048]{2,1,0:T(8,128)} copy(f32[1,1024,2048]{2,1,0:T(8,128)S(1)} %get-tuple-element.5) | data formatting | bytes 16777216

commit v3 on v0

v3 whole, which is shorter than its diff:
```python
import jax
import jax.numpy as jnp
from jax import lax
from jax.experimental import pallas as pl
from jax.experimental.pallas import tpu as pltpu
from jax.sharding import PartitionSpec as P

MESH = pl.DeviceIdType.MESH
BF16 = jnp.bfloat16
F32 = jnp.float32

QB = 128
CLIP_RMS = 0.1
OUTER_RATE = 0.7
MOMENTUM_RATE = 0.9
LEVELS = 127.0

NR = 8
NF = 16
PIECE = 128
HALF = 64
SPLIT = 896
LOOKAHEAD = 4


def kernel(
    loc_h, anc_h, ow_h, mo_h,
    ow, mo, blended,
    anc, dq, ra, relb, finb, rela, fina, xb, tot, toth, g,
    u, vx, w, oh, v, t, obuf, part, s1, part2, s2,
    ld, iosem, ss, rs, zs_sem, zr_sem, ps_sem, pr_sem, as_sem, ar_sem,
):
    rows, width = dq.shape
    loc = blended.at[0]
    r = lax.axis_index("replica")
    f = lax.axis_index("fsdp")
    xh, y = r // 4, r % 4
    z, xl, c = f // 4, (f // 2) % 2, f % 2
    chip = r * 2 + xl
    column = z * 2 + c
    yl, yr, yo = (y + 3) % 4, (y + 1) % 4, (y + 2) % 4
    left = (xh * 4 + yl, f)
    right = (xh * 4 + yr, f)
    across = ((1 - xh) * 4 + y, f)

    def row(x_of, y_of, offset=0):
        return pl.multiple_of((4 * x_of + y_of) * PIECE + offset, HALF)

    spans = ((0, SPLIT), (SPLIT, width - SPLIT))
    cols = [pl.ds(*span) for span in spans]

    far = 1 - xh
    units = [
        (far, yo, 1), (far, yo, 0), (far, yr, 1), (far, yl, 1), (far, yr, 0), (xh, yo, 1),
        (far, yl, 0), (xh, yr, 1), (xh, yl, 1), (far, y, 0), (far, y, 1), (xh, yo, 0),
        (xh, yr, 0), (xh, yl, 0), (xh, y, 1), (xh, y, 0),
    ]
    loads = []
    for k, unit in enumerate(units):
        at, where = pl.ds(row(*unit[:2]), PIECE), cols[unit[2]]
        loads.append(
            (
                pltpu.make_async_copy(loc_h.at[0, at, where], loc.at[at, where], ld.at[2 * k]),
                pltpu.make_async_copy(anc_h.at[at, where], anc.at[at, where], ld.at[2 * k + 1]),
            )
        )
    state_in = (
        pltpu.make_async_copy(ow_h, ow, iosem.at[0]),
        pltpu.make_async_copy(mo_h, mo, iosem.at[1]),
    )

    def begin(k):
        for copy in loads[k]:
            copy.start()

    begin(0)
    for copy in state_in:
        copy.start()
    for k in range(1, LOOKAHEAD):
        begin(k)

    barrier = pltpu.get_barrier_semaphore()

    def greet(*device):
        pl.semaphore_signal(barrier, inc=1, device_id=device, device_id_type=MESH)

    def greet_chip(i, _):
        other = (chip + i) % 16
        greet(other // 2, z * 4 + (other % 2) * 2 + c)
        return 0

    lax.fori_loop(1, 16, greet_chip, 0)
    for d in range(4):
        greet(xh * 4 + (y + d) % 4, z * 4 + xl * 2 + 1 - c)
    for d in (1, 2, 3):
        for c_of in (0, 1):
            greet(r, ((z + d) % 4) * 4 + xl * 2 + c_of)

    def quantize(k):
        for copy in loads[k]:
            copy.wait()
        if k + LOOKAHEAD < len(units):
            begin(k + LOOKAHEAD)
        base = row(*units[k][:2])
        first, count = spans[units[k][2]]

        def step(i, _):
            at = pl.ds(pl.multiple_of(base + i * 32, 32), 32)
            for b in range(first, first + count, QB):
                where = pl.ds(b, QB)
                block = anc[at, where].astype(F32) - loc[at, where]
                largest = jnp.max(jnp.abs(block), axis=1, keepdims=True)
                scale = ((largest + 1e-06) / LEVELS).astype(BF16).astype(F32)
                level = jnp.floor(block / scale + 0.5)
                dq[at, where] = (level * scale).astype(BF16)
            return 0

        lax.fori_loop(0, PIECE // 32, step, 0)

    def add(dst, side, terms, count):
        dst_ref, dst_base = dst

        def read(ref, at):
            return (ref[at, cols[side]] if ref is dq else ref[at, :]).astype(F32)

        def step(i, _):
            value = None
            for ref, base in terms:
                x = read(ref, pl.ds(pl.multiple_of(base + i * 16, 16), 16))
                value = x if value is None else value + x
            dst_ref[pl.ds(pl.multiple_of(dst_base + i * 16, 16), 16), cols[side]] = value.astype(BF16)
            return 0

        lax.fori_loop(0, count // 16, step, 0)

    def wait_bytes(ref, sem):
        pltpu.make_async_copy(ref, ref, sem).wait()

    sent = []

    def put(src, dst, device):
        k = len(sent)
        copy = pltpu.make_async_remote_copy(
            src_ref=src, dst_ref=dst, send_sem=ss.at[k], recv_sem=rs.at[k],
            device_id=device, device_id_type=MESH,
        )
        copy.start()
        sent.append(copy)
        return copy

    def prepare(i, _):
        at = pl.ds(pl.multiple_of(i * 128, 128), 128)
        oh[i // 8, i % 4, (i // 4) % 2] = (
            ow[at, :] - (OUTER_RATE * MOMENTUM_RATE * MOMENTUM_RATE) * mo[at, :]
        ).astype(BF16)
        return 0

    fb = [far, xh]
    ay = [yo, yr, yl, y]
    ra_copies, rela_copies, fina_copies, xb_copies = [], [], [], []
    relb_copies, finb_copies = [[], []], [[], []]
    carry = [jnp.zeros((8, 128), F32)]

    def send(base, side, count, dst, dst_base, device):
        return put(
            dq.at[pl.ds(base, count), cols[side]], dst.at[pl.ds(dst_base, count)], device
        )

    def far_b(j):
        base = row(fb[j], yo)
        relb_copies[j] = [
            send(base, 1, HALF, relb, j * PIECE, right),
            send(base + HALF, 1, HALF, relb, j * PIECE + HALF, left),
        ]

    def near_b(j):
        into = 2 * j * PIECE
        finb_copies[j].append(send(row(fb[j], yr, HALF), 1, HALF, finb, into + HALF, right))
        finb_copies[j].append(send(row(fb[j], yl), 1, HALF, finb, into + PIECE, left))

    def relay_b(j):
        into = 2 * j * PIECE
        relb_copies[j][0].wait_recv()
        base = row(fb[j], yr)
        add((dq, base), 1, ((dq, base), (relb, j * PIECE)), HALF)
        finb_copies[j].append(send(base, 1, HALF, finb, into, right))
        relb_copies[j][1].wait_recv()
        base = row(fb[j], yl, HALF)
        add((dq, base), 1, ((dq, base), (relb, j * PIECE + HALF)), HALF)
        finb_copies[j].append(send(base, 1, HALF, finb, into + PIECE + HALF, left))

    def sum_b():
        for copy in finb_copies[0]:
            copy.wait_recv()
        base = row(far, y)
        add((dq, base), 1, ((dq, base), (finb, 0), (finb, PIECE)), PIECE)
        xb_copies.append(send(base, 1, PIECE, xb, 0, across))

    def send_a(i):
        ra_copies.append(send(row(far, ay[i]), 0, PIECE, ra, i * PIECE, across))

    def pair_a(i):
        ra_copies[i].wait_recv()
        base = row(xh, ay[i])
        add((dq, base), 0, ((dq, base), (ra, i * PIECE)), PIECE)
        if i == 0:
            rela_copies.append(send(base, 0, HALF, rela, 0, right))
            rela_copies.append(send(base + HALF, 0, HALF, rela, HALF, left))
        elif i == 1:
            fina_copies.append(send(base + HALF, 0, HALF, fina, HALF, right))
        else:
            fina_copies.append(send(base, 0, HALF, fina, PIECE, left))

    def relay_a():
        rela_copies[0].wait_recv()
        base = row(xh, yr)
        add((dq, base), 0, ((dq, base), (rela, 0)), HALF)
        fina_copies.append(send(base, 0, HALF, fina, 0, right))
        rela_copies[1].wait_recv()
        base = row(xh, yl, HALF)
        add((dq, base), 0, ((dq, base), (rela, HALF)), HALF)
        fina_copies.append(send(base, 0, HALF, fina, PIECE + HALF, left))

    def total(side, terms):
        first, count = spans[side]

        def step(i, carry):
            at = pl.ds(pl.multiple_of(i * 16, 16), 16)
            value = dq[pl.ds(pl.multiple_of(row(xh, y) + i * 16, 16), 16), cols[side]].astype(F32)
            for ref, base in terms:
                value = value + ref[pl.ds(pl.multiple_of(base + i * 16, 16), 16), :].astype(F32)
            tot[at, cols[side]] = value
            square = value * value
            for b in range(0, count, 128):
                block = (first + b) // 128
                toth[block // 4, (block // 2) % 2, block % 2, at, :] = value[:, b : b + 128].astype(BF16)
                carry = carry + square[0:8, b : b + 128] + square[8:16, b : b + 128]
            return carry

        carry[0] = lax.fori_loop(0, PIECE // 16, step, carry[0])

    def total_b():
        for copy in finb_copies[1]:
            copy.wait_recv()
        xb_copies[0].wait_recv()
        total(1, ((finb, 2 * PIECE), (finb, 3 * PIECE), (xb, 0)))

    def total_a():
        ra_copies[3].wait_recv()
        for copy in fina_copies:
            copy.wait_recv()
        total(0, ((ra, 3 * PIECE), (fina, 0), (fina, PIECE)))

    def share(src, dst, q, own, device):
        @pl.when(own)
        def _():
            pltpu.make_async_copy(src, dst, pr_sem.at[q]).start()

        @pl.when(jnp.logical_not(own))
        def _():
            pltpu.make_async_remote_copy(
                src_ref=src, dst_ref=dst, send_sem=ps_sem.at[q], recv_sem=pr_sem.at[q],
                device_id=device, device_id_type=MESH,
            ).start()

    def prepare_state():
        for copy in state_in:
            copy.wait()
        lax.fori_loop(0, 16, prepare, 0)

    def state_y(b):
        c_of, y_of = b // 4, b % 4
        share(
            oh.at[c_of, y_of], v.at[y, :, c], 0,
            jnp.logical_and(y_of == y, c_of == c), (xh * 4 + y_of, z * 4 + xl * 2 + c_of),
        )

    def state_wait_y():
        wait_bytes(v, pr_sem.at[0])

    def state_x(b):
        x_of, y_of = b // 4, b % 4
        share(
            v.at[y_of, x_of], t.at[2 * xh + y_of // 2, xl], 2,
            jnp.logical_and(x_of == xh, y_of % 2 == xl), (x_of * 4 + y, z * 4 + (y_of % 2) * 2 + c),
        )

    def along_z(src_of, dst_of, q):
        for dz in (1, 2, 3):
            z_of = (z + dz) % 4
            pltpu.make_async_remote_copy(
                src_ref=src_of(z_of), dst_ref=dst_of(z), send_sem=zs_sem.at[q], recv_sem=zr_sem.at[q],
                device_id=(r, z_of * 4 + xl * 2 + c), device_id_type=MESH,
            ).start()
        pltpu.make_async_copy(src_of(z), dst_of(z), zr_sem.at[q]).start()

    def state_z():
        wait_bytes(t, pr_sem.at[2])
        along_z(lambda z_of: t.at[z_of], lambda z_of: obuf.at[z_of], 0)

    def greeted():
        pl.semaphore_wait(barrier, 25)

    def run(steps):
        for step in steps:
            if isinstance(step, tuple):
                step[0](*step[1:])
            else:
                step()

    def quantize_each(*ks):
        for k in ks:
            quantize(k)

    def state_y_each(*bs):
        for b in bs:
            state_y(b)

    def state_x_each(*bs):
        for b in bs:
            state_x(b)

    run((
        prepare_state, (quantize, 0), greeted, (far_b, 0), (state_y_each, *range(8)),
        (quantize, 1), (send_a, 0), (quantize_each, 2, 3), (near_b, 0), (quantize, 4), (send_a, 1),
        (quantize, 5), (far_b, 1), (quantize, 6), (send_a, 2), (quantize_each, 7, 8), (near_b, 1),
        state_wait_y, (state_x_each, *range(8)), (relay_b, 0), (quantize, 9), (send_a, 3),
        (quantize_each, 10, 11), (pair_a, 0), (quantize_each, 12, 13), (relay_b, 1),
        (quantize_each, 14, 15), sum_b, state_z, (pair_a, 1), (pair_a, 2), relay_a, total_b, total_a,
    ))
    carry = carry[0]

    part[...] = carry
    s1[pl.ds(pl.multiple_of(chip * 8, 8), 8), :] = carry

    def tell_plane(i, _):
        other = (chip + i) % 16
        pltpu.make_async_remote_copy(
            src_ref=part, dst_ref=s1.at[pl.ds(pl.multiple_of(chip * 8, 8), 8)],
            send_sem=as_sem.at[0], recv_sem=ar_sem.at[0],
            device_id=(other // 2, z * 4 + (other % 2) * 2 + c), device_id_type=MESH,
        ).start()
        return 0

    lax.fori_loop(1, 16, tell_plane, 0)

    along_z(
        lambda z_of: toth.at[z_of],
        lambda z_of: u.at[z_of],
        1,
    )

    wait_bytes(s1.at[pl.ds(0, 15 * 8)], ar_sem.at[0])
    wait_bytes(s1.at[pl.ds(0, 15 * 8)], as_sem.at[0])
    in_plane = s1[0:8, :]
    for k in range(1, 16):
        in_plane = in_plane + s1[8 * k : 8 * k + 8, :]
    part2[...] = in_plane
    s2[pl.ds(pl.multiple_of(column * 8, 8), 8), :] = in_plane
    for d in range(1, 8):
        other = (column + d) % 8
        pltpu.make_async_remote_copy(
            src_ref=part2, dst_ref=s2.at[pl.ds(pl.multiple_of(column * 8, 8), 8)],
            send_sem=as_sem.at[1], recv_sem=ar_sem.at[1],
            device_id=(r, (other // 2) * 4 + xl * 2 + other % 2), device_id_type=MESH,
        ).start()
    wait_bytes(obuf, zr_sem.at[0])
    wait_bytes(s2.at[pl.ds(0, 56)], ar_sem.at[1])
    wait_bytes(s2.at[pl.ds(0, 56)], as_sem.at[1])
    everywhere = s2[0:8, :]
    for k in range(1, 8):
        everywhere = everywhere + s2[8 * k : 8 * k + 8, :]
    squares = jnp.sum(everywhere, keepdims=True)
    entries = float(rows * NF) * width
    mean = squares * (1.0 / (NR * NR * entries))
    factor = jnp.minimum(1.0, CLIP_RMS / jnp.sqrt(mean + 1e-06)) * (1.0 / NR)
    weight = (OUTER_RATE * (1.0 + MOMENTUM_RATE)) * factor

    own = row(xh, y)

    def outer_half(side):
        first, count = spans[side]

        def step(i, _):
            at = pl.ds(pl.multiple_of(i * 16, 16), 16)
            to = pl.ds(pl.multiple_of(own + i * 16, 16), 16)
            for b in range(first, first + count, 128):
                block = b // 128
                state = obuf[block // 4, (block // 2) % 2, block % 2, at, :]
                g[to, pl.ds(b, 128)] = (state.astype(F32) - weight * tot[at, pl.ds(b, 128)]).astype(BF16)
            return 0

        lax.fori_loop(0, PIECE // 16, step, 0)

    def move(base, count, side, device):
        part = g.at[pl.ds(pl.multiple_of(base, HALF), count), cols[side]]
        return put(part, part, device)

    def ring(x_of, side):
        base = row(x_of, y)
        r0 = move(base, HALF, side, right)
        l1 = move(base + HALF, HALF, side, left)
        r1 = move(base + HALF, HALF, side, right)
        l0 = move(base, HALF, side, left)
        return r0, l1, r1, l0

    def pass_on(x_of, side, copies):
        copies[0].wait_recv()
        first = move(row(x_of, yl), HALF, side, right)
        copies[1].wait_recv()
        second = move(row(x_of, yr, HALF), HALF, side, left)
        return first, second

    def value_x(x_of, x_lo):
        share(
            u.at[pl.ds(2 * x_of, 2), x_lo], vx.at[xh, xl], 1,
            jnp.logical_and(x_of == xh, x_lo == xl), (x_of * 4 + y, z * 4 + x_lo * 2 + c),
        )

    def value_y(y_of, c_of):
        share(
            vx.at[:, y_of % 2, y_of // 2, c_of], w.at[c, :, y], 3,
            jnp.logical_and(y_of == y, c_of == c), (xh * 4 + y_of, z * 4 + xl * 2 + c_of),
        )

    def blend(x_of, y_of, side):
        base = row(x_of, y_of)

        def step(i, _):
            at = pl.ds(pl.multiple_of(base + i * 32, 32), 32)
            loc[at, cols[side]] = 0.5 * loc[at, cols[side]] + 0.5 * g[at, cols[side]].astype(F32)
            return 0

        lax.fori_loop(0, PIECE // 32, step, 0)

    def finish(i, _):
        at = pl.ds(pl.multiple_of(i * 128, 128), 128)
        clipped = factor * w[i // 8, (i // 4) % 2, i % 4].astype(F32)
        momentum = MOMENTUM_RATE * mo[at, :] + clipped
        ow[at, :] = ow[at, :] - OUTER_RATE * (clipped + MOMENTUM_RATE * momentum)
        mo[at, :] = momentum
        return 0

    outer_half(1)
    over_b = move(own, PIECE, 1, across)
    outer_half(0)
    ring_a = ring(xh, 0)
    over_a = [move(own, PIECE, 0, across)]
    ring_b = ring(xh, 1)
    wait_bytes(u, zr_sem.at[1])
    for x_of in (0, 1):
        for x_lo in (0, 1):
            value_x(x_of, x_lo)
    blend(xh, y, 1)
    blend(xh, y, 0)
    on_a = pass_on(xh, 0, ring_a)
    ring_a[2].wait_recv()
    over_a.append(move(row(xh, yl), PIECE, 0, across))
    ring_a[3].wait_recv()
    over_a.append(move(row(xh, yr), PIECE, 0, across))
    blend(xh, yl, 0)
    blend(xh, yr, 0)
    over_b.wait_recv()
    ring_x = ring(far, 1)
    blend(far, y, 1)
    on_b = pass_on(xh, 1, ring_b)
    for copy in on_a:
        copy.wait_recv()
    over_a.append(move(row(xh, yo), PIECE, 0, across))
    blend(xh, yo, 0)
    wait_bytes(vx, pr_sem.at[1])
    for y_of in range(4):
        for c_of in (0, 1):
            value_y(y_of, c_of)
    for copy in ring_b[2:]:
        copy.wait_recv()
    blend(xh, yl, 1)
    blend(xh, yr, 1)
    over_a[0].wait_recv()
    blend(far, y, 0)
    on_x = pass_on(far, 1, ring_x)
    for copy in on_b:
        copy.wait_recv()
    blend(xh, yo, 1)
    for copy in ring_x[2:]:
        copy.wait_recv()
    blend(far, yl, 1)
    blend(far, yr, 1)
    over_a[1].wait_recv()
    blend(far, yl, 0)
    over_a[2].wait_recv()
    blend(far, yr, 0)
    wait_bytes(w, pr_sem.at[3])
    lax.fori_loop(0, 16, finish, 0)
    for copy in on_x:
        copy.wait_recv()
    blend(far, yo, 1)
    over_a[3].wait_recv()
    blend(far, yo, 0)

    for copy in sent:
        copy.wait_send()
    wait_bytes(t.at[pl.ds(0, 3)], zs_sem.at[0])
    wait_bytes(t.at[pl.ds(0, 3)], zs_sem.at[1])
    wait_bytes(oh.at[0, pl.ds(0, 3)], ps_sem.at[0])
    wait_bytes(oh.at[1], ps_sem.at[0])
    wait_bytes(t.at[pl.ds(0, 3)], ps_sem.at[1])
    wait_bytes(t.at[pl.ds(0, 3)], ps_sem.at[2])
    wait_bytes(oh.at[0, pl.ds(0, 3)], ps_sem.at[3])
    wait_bytes(oh.at[1], ps_sem.at[3])


def on_device(local_weights, anchor, outer_weights, momentum):
    _, rows, width = local_weights.shape
    owned, tile = outer_weights.shape
    whole = pl.BlockSpec(memory_space=pl.ANY)
    vmem = pltpu.VMEM
    dma = pltpu.SemaphoreType.DMA
    return pl.pallas_call(
        kernel,
        out_shape=(
            vmem((owned, tile), F32),
            vmem((owned, tile), F32),
            vmem((1, rows, width), F32),
        ),
        in_specs=[whole] * 4,
        out_specs=(pl.BlockSpec(memory_space=vmem),) * 3,
        scratch_shapes=[
            vmem((rows, width), BF16),
            vmem((rows, width), BF16),
            vmem((4 * PIECE, SPLIT), BF16),
            vmem((2 * PIECE, width - SPLIT), BF16),
            vmem((4 * PIECE, width - SPLIT), BF16),
            vmem((PIECE, SPLIT), BF16),
            vmem((2 * PIECE, SPLIT), BF16),
            vmem((PIECE, width - SPLIT), BF16),
            vmem((PIECE, width), F32),
            vmem((4, 2, 2, PIECE, 128), BF16),
            vmem((rows, width), BF16),
            vmem((4, 2, 2, PIECE, 128), BF16),
            vmem((2, 2, 2, 2, PIECE, 128), BF16),
            vmem((2, 2, 4, PIECE, 128), BF16),
            vmem((2, 4, 2, PIECE, 128), BF16),
            vmem((4, 2, 2, PIECE, 128), BF16),
            vmem((4, 2, 2, PIECE, 128), BF16),
            vmem((4, 2, 2, PIECE, 128), BF16),
            vmem((8, 128), F32),
            vmem((128, 128), F32),
            vmem((8, 128), F32),
            vmem((64, 128), F32),
            dma((32,)),
            dma((2,)),
            dma((64,)),
            dma((64,)),
            dma((2,)),
            dma((2,)),
            dma((4,)),
            dma((4,)),
            dma((2,)),
            dma((2,)),
        ],
        compiler_params=pltpu.CompilerParams(
            collective_id=0, has_side_effects=True, vmem_limit_bytes=36 << 20
        ),
    )(*(pltpu.with_memory_space_constraint(a, pltpu.HBM) for a in (local_weights, anchor, outer_weights, momentum)))


def solution(mesh):
    placed = (
        P("replica", "fsdp", None),
        P("fsdp", None),
        P("replica", "fsdp"),
        P("replica", "fsdp"),
    )
    return jax.shard_map(
        on_device,
        mesh=mesh,
        in_specs=placed,
        out_specs=(P("replica", "fsdp"), P("replica", "fsdp"), P("replica", "fsdp", None)),
        check_vma=False,
    )
```

time: 456 us -> 95 us (0.21)
  waiting for transfers between devices: 271 us -> 0 us
  Pallas kernels: 0 us -> 89 us
  blocking collectives: 65 us -> 0 us
  other arithmetic: 51.8 us -> 0 us
  local copies, waits for them, and re-layouts: 33.8 us -> 5.34 us
  starting transfers between devices: 19.1 us -> 0 us
  between operations: 14.8 us -> 0.64 us
    reduce_scatter x1 -> x0, waiting for transfers between devices: 114 us -> none  [on_device(): lax.psum_scatter(dequantize(column_quant, column_scales, QB), 'replica',...]
    all_to_all x3 -> x0, waiting for transfers between devices: 90 us -> none  [the longest x1 49.5 us: on_device(): lax.all_to_all(quantized, 'fsdp', split_axis=1, concat_axis=0, tiled=True)]
    pallas_call x0 -> x1, Pallas kernels: none -> 89 us  [on_device(): pl.pallas_call(kernel, out_shape=(vmem((owned, tile), F32), vmem((owned,...]
    all_gather x1 -> x0, waiting for transfers between devices: 67.4 us -> none  [on_device(): stacked = lax.all_gather(outer_half, 'replica', axis=0, tiled=True)]
    psum x1 -> x0, blocking collectives: 65 us -> none  [on_device(): squares = lax.psum(jnp.sum(average * average), ('replica', 'fsdp'))]
    unnamed x12 -> x3, local copies, waits for them, and re-layouts: 24.9 us -> 5.34 us
    all_to_all x3 -> x0, starting transfers between devices: 19 us -> none  [the longest x1 7.76 us: on_device(): lax.all_to_all(scales_half, 'fsdp', split_axis=1, concat_axis=0, tiled=True)]
    add x1 -> x0, other arithmetic: 12 us -> none  [on_device(): blended = 0.5 * local_rows + 0.5 * returned.astype(jnp.float32)]
  transfers between devices with their start and end apart: 5 -> 0, of which waited for: 4 -> 0; matrix products, arithmetic and copies ran while one was open for 4% -> 0% of each run, Pallas kernels for 0% -> 0%
where the time goes in v3:
time: 95 us; the launch traced here: 94.9 us
  Pallas kernels  89 us (94%)
  local copies, waits for them, and re-layouts  5.34 us (6%)
    pallas_call x1, Pallas kernels, on_device(): pl.pallas_call(kernel, out_shape=(vmem((owned, tile), F32), vmem((owned,...  89 us
    unnamed x3, local copies, waits for them, and re-layouts  5.34 us

profile of v3, /device:TPU:1, one launch (start us, length us, event | category | flops | bytes accessed | tf_op | source)
XLA Modules:
  0.0 94.9 jit_solution(2940649651903013940)
XLA Ops:
  0.6 89.0 %shard_map.67 = (f32[2048,128]{1,0:T(8,128)S(1)}, f32[2048,128]{1,0:T(8,128)S(1)}, f32[1,1024,2048]{2,1,0:T(8,128)S(1)}) custom-call(f32[1,1024,2048]{2,1,0:T(8,128)} %loc_h.1, bf16[1024,2048]{1,0:T(8,128)(2,1)} %anc_h.1, f32[2048,128]{1,0:T(8,128)} %ow_h.1, f32[2048,128]{1,0:T(8,128)} %mo_h.1), custom_call_target="tpu_custom_call" | custom-call | tf_op jit(solution)/shard_map/pallas_call | solution.py:519
  89.6 1.0 %copy.10 = f32[2048,128]{1,0:T(8,128)} copy(f32[2048,128]{1,0:T(8,128)S(1)} %get-tuple-element.3) | data formatting | bytes 2097152
  90.6 1.0 %copy.11 = f32[2048,128]{1,0:T(8,128)} copy(f32[2048,128]{1,0:T(8,128)S(1)} %get-tuple-element.4) | data formatting | bytes 2097152
  91.5 3.4 %copy.12 = f32[1,1024,2048]{2,1,0:T(8,128)} copy(f32[1,1024,2048]{2,1,0:T(8,128)S(1)} %get-tuple-element.5) | data formatting | bytes 16777216

commit v4 on v3

--- a/solution.py
+++ b/solution.py
@@ -20,6 +20,7 @@
 PIECE = 128
 HALF = 64
 SPLIT = 896
+BACK = 896
 LOOKAHEAD = 4
 
 
@@ -48,6 +49,8 @@
 
     spans = ((0, SPLIT), (SPLIT, width - SPLIT))
     cols = [pl.ds(*span) for span in spans]
+    back_spans = ((0, BACK), (BACK, width - BACK))
+    back = [pl.ds(*span) for span in back_spans]
 
     far = 1 - xh
     units = [
@@ -321,8 +324,8 @@
             state_x(b)
 
     run((
-        prepare_state, (quantize, 0), greeted, (far_b, 0), (state_y_each, *range(8)),
-        (quantize, 1), (send_a, 0), (quantize_each, 2, 3), (near_b, 0), (quantize, 4), (send_a, 1),
+        prepare_state, (quantize, 0), greeted, (far_b, 0),
+        (quantize, 1), (send_a, 0), (quantize_each, 2, 3), (near_b, 0), (state_y_each, *range(8)), (quantize, 4), (send_a, 1),
         (quantize, 5), (far_b, 1), (quantize, 6), (send_a, 2), (quantize_each, 7, 8), (near_b, 1),
         state_wait_y, (state_x_each, *range(8)), (relay_b, 0), (quantize, 9), (send_a, 3),
         (quantize_each, 10, 11), (pair_a, 0), (quantize_each, 12, 13), (relay_b, 1),
@@ -333,25 +336,19 @@
     part[...] = carry
     s1[pl.ds(pl.multiple_of(chip * 8, 8), 8), :] = carry
 
-    def tell_plane(i, _):
-        other = (chip + i) % 16
+    def tell_chip(d):
+        x_of, y_of = (2 * xh + xl + d // 4) % 4, (y + d) % 4
         pltpu.make_async_remote_copy(
             src_ref=part, dst_ref=s1.at[pl.ds(pl.multiple_of(chip * 8, 8), 8)],
             send_sem=as_sem.at[0], recv_sem=ar_sem.at[0],
-            device_id=(other // 2, z * 4 + (other % 2) * 2 + c), device_id_type=MESH,
+            device_id=((x_of // 2) * 4 + y_of, z * 4 + (x_of % 2) * 2 + c), device_id_type=MESH,
         ).start()
-        return 0
-
-    lax.fori_loop(1, 16, tell_plane, 0)
-
-    along_z(
-        lambda z_of: toth.at[z_of],
-        lambda z_of: u.at[z_of],
-        1,
-    )
+
+    for d in (13, 14, 15, 9, 10, 11, 5, 6, 7, 12, 8, 4, 1, 2, 3):
+        tell_chip(d)
+
 
     wait_bytes(s1.at[pl.ds(0, 15 * 8)], ar_sem.at[0])
-    wait_bytes(s1.at[pl.ds(0, 15 * 8)], as_sem.at[0])
     in_plane = s1[0:8, :]
     for k in range(1, 16):
         in_plane = in_plane + s1[8 * k : 8 * k + 8, :]
@@ -366,7 +363,6 @@
         ).start()
     wait_bytes(obuf, zr_sem.at[0])
     wait_bytes(s2.at[pl.ds(0, 56)], ar_sem.at[1])
-    wait_bytes(s2.at[pl.ds(0, 56)], as_sem.at[1])
     everywhere = s2[0:8, :]
     for k in range(1, 8):
         everywhere = everywhere + s2[8 * k : 8 * k + 8, :]
@@ -379,7 +375,7 @@
     own = row(xh, y)
 
     def outer_half(side):
-        first, count = spans[side]
+        first, count = back_spans[side]
 
         def step(i, _):
             at = pl.ds(pl.multiple_of(i * 16, 16), 16)
@@ -393,7 +389,7 @@
         lax.fori_loop(0, PIECE // 16, step, 0)
 
     def move(base, count, side, device):
-        part = g.at[pl.ds(pl.multiple_of(base, HALF), count), cols[side]]
+        part = g.at[pl.ds(pl.multiple_of(base, HALF), count), back[side]]
         return put(part, part, device)
 
     def ring(x_of, side):
@@ -428,7 +424,7 @@
 
         def step(i, _):
             at = pl.ds(pl.multiple_of(base + i * 32, 32), 32)
-            loc[at, cols[side]] = 0.5 * loc[at, cols[side]] + 0.5 * g[at, cols[side]].astype(F32)
+            loc[at, back[side]] = 0.5 * loc[at, back[side]] + 0.5 * g[at, back[side]].astype(F32)
             return 0
 
         lax.fori_loop(0, PIECE // 32, step, 0)
@@ -447,6 +443,11 @@
     ring_a = ring(xh, 0)
     over_a = [move(own, PIECE, 0, across)]
     ring_b = ring(xh, 1)
+    along_z(
+        lambda z_of: toth.at[z_of],
+        lambda z_of: u.at[z_of],
+        1,
+    )
     wait_bytes(u, zr_sem.at[1])
     for x_of in (0, 1):
         for x_lo in (0, 1):
@@ -497,6 +498,8 @@
     blend(far, yo, 1)
     over_a[3].wait_recv()
     blend(far, yo, 0)
+    wait_bytes(s1.at[pl.ds(0, 15 * 8)], as_sem.at[0])
+    wait_bytes(s2.at[pl.ds(0, 56)], as_sem.at[1])
 
     for copy in sent:
         copy.wait_send()

time: 95 us -> 94.4 us (level)
  no operation moved by 1% of the time
where the time goes in v4:
time: 94.4 us; the launch traced here: 94.3 us
  Pallas kernels  88.3 us (94%)
  local copies, waits for them, and re-layouts  5.34 us (6%)
    pallas_call x1, Pallas kernels, on_device(): pl.pallas_call(kernel, out_shape=(vmem((owned, tile), F32), vmem((owned,...  88.3 us
    unnamed x3, local copies, waits for them, and re-layouts  5.34 us

profile of v4, /device:TPU:1, one launch (start us, length us, event | category | flops | bytes accessed | tf_op | source)
XLA Modules:
  0.0 94.3 jit_solution(7288737234107474079)
XLA Ops:
  0.6 88.3 %shard_map.67 = (f32[2048,128]{1,0:T(8,128)S(1)}, f32[2048,128]{1,0:T(8,128)S(1)}, f32[1,1024,2048]{2,1,0:T(8,128)S(1)}) custom-call(f32[1,1024,2048]{2,1,0:T(8,128)} %loc_h.1, bf16[1024,2048]{1,0:T(8,128)(2,1)} %anc_h.1, f32[2048,128]{1,0:T(8,128)} %ow_h.1, f32[2048,128]{1,0:T(8,128)} %mo_h.1), custom_call_target="tpu_custom_call" | custom-call | tf_op jit(solution)/shard_map/pallas_call | solution.py:522
  88.9 1.0 %copy.10 = f32[2048,128]{1,0:T(8,128)} copy(f32[2048,128]{1,0:T(8,128)S(1)} %get-tuple-element.3) | data formatting | bytes 2097152
  89.9 1.0 %copy.11 = f32[2048,128]{1,0:T(8,128)} copy(f32[2048,128]{1,0:T(8,128)S(1)} %get-tuple-element.4) | data formatting | bytes 2097152
  90.9 3.4 %copy.12 = f32[1,1024,2048]{2,1,0:T(8,128)} copy(f32[1,1024,2048]{2,1,0:T(8,128)S(1)} %get-tuple-element.5) | data formatting | bytes 16777216

commit v5 on v4

--- a/solution.py
+++ b/solution.py
@@ -26,9 +26,9 @@
 
 def kernel(
     loc_h, anc_h, ow_h, mo_h,
-    ow, mo, blended,
+    clip_out, blended,
     anc, dq, ra, relb, finb, rela, fina, xb, tot, toth, g,
-    u, vx, w, oh, v, t, obuf, part, s1, part2, s2,
+    u, vx, w, ow, mo, oh, v, t, obuf, part, s1, part2, s2,
     ld, iosem, ss, rs, zs_sem, zr_sem, ps_sem, pr_sem, as_sem, ar_sem,
 ):
     rows, width = dq.shape
@@ -431,10 +431,7 @@
 
     def finish(i, _):
         at = pl.ds(pl.multiple_of(i * 128, 128), 128)
-        clipped = factor * w[i // 8, (i // 4) % 2, i % 4].astype(F32)
-        momentum = MOMENTUM_RATE * mo[at, :] + clipped
-        ow[at, :] = ow[at, :] - OUTER_RATE * (clipped + MOMENTUM_RATE * momentum)
-        mo[at, :] = momentum
+        clip_out[at, :] = factor * w[i // 8, (i // 4) % 2, i % 4].astype(F32)
         return 0
 
     outer_half(1)
@@ -519,15 +516,14 @@
     whole = pl.BlockSpec(memory_space=pl.ANY)
     vmem = pltpu.VMEM
     dma = pltpu.SemaphoreType.DMA
-    return pl.pallas_call(
+    clipped, blended = pl.pallas_call(
         kernel,
         out_shape=(
-            vmem((owned, tile), F32),
             vmem((owned, tile), F32),
             vmem((1, rows, width), F32),
         ),
         in_specs=[whole] * 4,
-        out_specs=(pl.BlockSpec(memory_space=vmem),) * 3,
+        out_specs=(pl.BlockSpec(memory_space=vmem),) * 2,
         scratch_shapes=[
             vmem((rows, width), BF16),
             vmem((rows, width), BF16),
@@ -543,6 +539,8 @@
             vmem((4, 2, 2, PIECE, 128), BF16),
             vmem((2, 2, 2, 2, PIECE, 128), BF16),
             vmem((2, 2, 4, PIECE, 128), BF16),
+            vmem((owned, tile), F32),
+            vmem((owned, tile), F32),
             vmem((2, 4, 2, PIECE, 128), BF16),
             vmem((4, 2, 2, PIECE, 128), BF16),
             vmem((4, 2, 2, PIECE, 128), BF16),
@@ -566,6 +564,9 @@
             collective_id=0, has_side_effects=True, vmem_limit_bytes=36 << 20
         ),
     )(*(pltpu.with_memory_space_constraint(a, pltpu.HBM) for a in (local_weights, anchor, outer_weights, momentum)))
+    new_momentum = MOMENTUM_RATE * momentum + clipped
+    new_outer = outer_weights - OUTER_RATE * (clipped + MOMENTUM_RATE * new_momentum)
+    return new_outer, new_momentum, blended
 
 
 def solution(mesh):

time: 94.4 us -> 94.2 us (level)
  local copies, waits for them, and re-layouts: 5.34 us -> 3.4 us
  other arithmetic: 0 us -> 1.56 us
    unnamed x3 -> x5, local copies, waits for them, and re-layouts: 5.34 us -> 3.4 us
    sub x0 -> x1, other arithmetic: none -> 1.56 us  [on_device(): outer_weights - OUTER_RATE * (clipped + MOMENTUM_RATE * new_momentum)]
where the time goes in v5:
time: 94.2 us; the launch traced here: 94.1 us
  Pallas kernels  88.4 us (94%)
  local copies, waits for them, and re-layouts  3.4 us (4%)
  other arithmetic  1.56 us (2%)
    pallas_call x1, Pallas kernels, on_device(): pl.pallas_call(kernel, out_shape=(vmem((owned, tile), F32), vmem((1, rows...  88.4 us
    unnamed x5, local copies, waits for them, and re-layouts  3.4 us

profile of v5, /device:TPU:1, one launch (start us, length us, event | category | flops | bytes accessed | tf_op | source)
XLA Modules:
  0.0 94.1 jit_solution(10135806994653285252)
XLA Ops:
  0.6 0.0 copy-start.1
  0.6 0.0 copy-start
  0.7 88.4 %shard_map.67 = (f32[2048,128]{1,0:T(8,128)S(1)}, f32[1,1024,2048]{2,1,0:T(8,128)S(1)}) custom-call(f32[1,1024,2048]{2,1,0:T(8,128)} %loc_h.1, bf16[1024,2048]{1,0:T(8,128)(2,1)} %anc_h.1, f32[2048,128]{1,0:T(8,128)} %ow_h.1, f32[2048,128]{1,0:T(8,128)} %mo_h.1), custom_call_target="tpu_custom_call" | custom-call | tf_op jit(solution)/shard_map/pallas_call | solution.py:519
  89.1 0.0 copy-done.1
  89.1 0.0 copy-done
  89.1 1.6 %multiply_subtract_fusion = (f32[2048,128]{1,0:T(8,128)}, f32[2048,128]{1,0:T(8,128)}) fusion(f32[2048,128]{1,0:T(8,128)S(1)} %copy-done, f32[2048,128]{1,0:T(8,128)S(1)} %get-tuple-element.5, f32[2048,128]{1,0:T(8,128)S(1)} %copy-done.1), kind=kLoop, calls=%fused_computation | loop fusion | flops 1572864 | bytes 5242880 | tf_op jit(solution)/shard_map/sub | solution.py:568
  90.7 3.4 %copy.8 = f32[1,1024,2048]{2,1,0:T(8,128)} copy(f32[1,1024,2048]{2,1,0:T(8,128)S(1)} %get-tuple-element.11) | data formatting | bytes 16777216
Async XLA Ops:
  0.6 88.5 %copy-start.1 = (f32[2048,128]{1,0:T(8,128)S(1)}, f32[2048,128]{1,0:T(8,128)}, u32[]{:S(2)}) copy-start(f32[2048,128]{1,0:T(8,128)} %mo_h.1) | copy-start | bytes 3145732
  0.6 88.5 %copy-start = (f32[2048,128]{1,0:T(8,128)S(1)}, f32[2048,128]{1,0:T(8,128)}, u32[]{:S(2)}) copy-start(f32[2048,128]{1,0:T(8,128)} %ow_h.1) | copy-start | bytes 3145732
